TPU v7x, 256 devices: a whole 4x4x8 slice. The times are simulated.
256 devices in a mesh: dom: 4 (over y_lo, core), dev: 64 (over x, y_hi, z).
Axes of the slice: x: 4, y: 4 (y_hi: 2, y_lo: 2; y = y_hi * 2 + y_lo), z: 8, core: 2. Of those that a mesh axis runs over, the one named last changes fastest.
Arguments:
- features: bfloat16 [262144, 256], P(('dom', 'dev')), may hold values from -6 to 6
- weight: bfloat16 [256, 256], replicated, may hold values from -0.375 to 0.375
- cotangent: bfloat16 [262144, 256], P(('dom', 'dev')), may hold values from -6 to 6
- send_list: int32 [4, 64, 64, 1], P('dom', 'dev'), may hold values from 0 to 7
- intra_rows: int32 [4, 64, 32], P('dom', 'dev'), may hold values from 0 to 7
- intra_src: int32 [4, 64, 32], P('dom', 'dev'), may hold values from 0 to 63
- intra_count: int32 [4, 64], P('dom', 'dev'), may hold values from 8 to 32, as said below
- intra_vals: bfloat16 [4, 64, 32, 128, 128], P('dom', 'dev'), may hold values from -0.15625 to 0.15625
- cross_rows: int32 [4, 64, 3, 16], P('dom', 'dev'), may hold values from 0 to 7
- cross_cols: int32 [4, 64, 3, 16], P('dom', 'dev'), may hold values from 0 to 7
- cross_vals: bfloat16 [4, 64, 3, 16, 128, 128], P('dom', 'dev'), may hold values from -0.15625 to 0.15625
Outputs:
- activated: bfloat16 [262144, 256], P(('dom', 'dev'))
- input_grad: bfloat16 [262144, 256], P(('dom', 'dev'))
- weight_grad: float32 [256, 256], replicated
Inputs may be any that keep to these rules, and one draw needn't show every extreme that they name: `intra_count`: each device has from 8 to 32 live tiles inside its partition; some device has exactly 32.
All inputs are finite; a program needn't handle non-finite values.
Results may differ from a plain program's by a relative error of at most 0.0061.
Values may be sent and summed in bfloat16 or wider, within the bound.
A program may use at most 128 MiB of HBM per device.

v0:
```python
import math

import jax
import jax.numpy as jnp
from jax import lax
from jax.sharding import PartitionSpec as P


def from_behind(value, axis, steps):
    count = lax.axis_size(axis)
    pairs = [(source, (source + steps) % count) for source in range(count)]
    return lax.ppermute(value, axis, pairs)


def body(
    features,
    weight,
    cotangent,
    send_list,
    intra_rows,
    intra_src,
    intra_count,
    intra_vals,
    cross_rows,
    cross_cols,
    cross_vals,
):
    rows_total, feat_width = features.shape
    block_rows = intra_vals.shape[-1]
    block_count = rows_total // block_rows
    own_blocks = features.reshape(block_count, block_rows, feat_width)
    dev_count = lax.axis_size("dev")
    dom_count = lax.axis_size("dom")
    send_slots = send_list[0, 0]
    slot_count = send_slots.shape[1]
    flat_slots = send_slots.reshape(-1)
    tile_rows = intra_rows[0, 0]
    tile_source = intra_src[0, 0]
    tile_count = tile_rows.shape[0]
    live_mask = (jnp.arange(tile_count) < intra_count[0, 0]).astype(jnp.bfloat16)
    tile_vals = intra_vals[0, 0] * live_mask[:, None, None]
    cross_row = cross_rows[0, 0]
    cross_col = cross_cols[0, 0]
    cross_val = cross_vals[0, 0]
    zero_blocks = jnp.zeros((block_count, block_rows, feat_width), jnp.float32)
    outgoing = own_blocks[flat_slots].reshape(dev_count, slot_count, block_rows, feat_width)
    incoming = lax.all_to_all(outgoing, "dev", split_axis=0, concat_axis=0, tiled=True)
    slot_pool = incoming.reshape(dev_count * slot_count, block_rows, feat_width)
    contrib = jnp.einsum(
        "kab,kbf->kaf", tile_vals, slot_pool[tile_source], preferred_element_type=jnp.float32
    )
    summed = zero_blocks.at[tile_rows].add(contrib)
    remote = own_blocks
    for offset in range(1, dom_count):
        remote = from_behind(remote, "dom", 1)
        cross_group = offset - 1
        cross_cross_out = jnp.einsum(
            "kab,kbf->kaf",
            cross_val[cross_group],
            remote[cross_col[cross_group]],
            preferred_element_type=jnp.float32,
        )
        summed = summed.at[cross_row[cross_group]].add(cross_cross_out)
    aggregated = summed.reshape(rows_total, feat_width).astype(jnp.bfloat16)
    pre_act = jnp.dot(aggregated, weight, preferred_element_type=jnp.float32)
    activated = jax.nn.silu(pre_act).astype(jnp.bfloat16)
    sigmoid_v = jax.nn.sigmoid(pre_act)
    pre_grad = (
        cotangent.astype(jnp.float32) * sigmoid_v * (1.0 + pre_act * (1.0 - sigmoid_v))
    ).astype(jnp.bfloat16)
    partial_weight = lax.dot_general(
        aggregated, pre_grad, (((0,), (0,)), ((), ())), preferred_element_type=jnp.float32
    )
    grad_scale = 1.0 / math.sqrt(rows_total * dev_count * dom_count)
    weight_sum_all = lax.psum(partial_weight, ("dom", "dev"))
    weight_grad = weight_sum_all * grad_scale
    back_grad = lax.dot_general(
        pre_grad, weight, (((1,), (1,)), ((), ())), preferred_element_type=jnp.float32
    ).astype(jnp.bfloat16)
    back_blocks = back_grad.reshape(block_count, block_rows, feat_width)
    tile_back = jnp.einsum(
        "kab,kaf->kbf", tile_vals, back_blocks[tile_rows], preferred_element_type=jnp.float32
    )
    slot_sums = (
        jnp.zeros((dev_count * slot_count, block_rows, feat_width), jnp.float32)
        .at[tile_source]
        .add(tile_back)
    )
    slot_sums = slot_sums.reshape(dev_count, slot_count, block_rows, feat_width)
    returned = lax.all_to_all(slot_sums, "dev", split_axis=0, concat_axis=0, tiled=True)
    input_grad = zero_blocks.at[flat_slots].add(
        returned.reshape(dev_count * slot_count, block_rows, feat_width)
    )
    carried = zero_blocks
    for offset in range(dom_count - 1, 0, -1):
        group = offset - 1
        cross_out = jnp.einsum(
            "kab,kaf->kbf",
            cross_val[group],
            back_blocks[cross_row[group]],
            preferred_element_type=jnp.float32,
        )
        carried = from_behind(carried + zero_blocks.at[cross_col[group]].add(cross_out), "dom", -1)
    input_grad = input_grad + carried
    return (activated, input_grad.reshape(rows_total, feat_width).astype(jnp.bfloat16), weight_grad)


def solution(mesh):
    placed = (
        P(("dom", "dev"), None),
        P(),
        P(("dom", "dev"), None),
        P("dom", "dev", None, None),
        P("dom", "dev", None),
        P("dom", "dev", None),
        P("dom", "dev"),
        P("dom", "dev", None, None, None),
        P("dom", "dev", None, None),
        P("dom", "dev", None, None),
        P("dom", "dev", None, None, None, None),
    )
    return jax.shard_map(
        body,
        mesh=mesh,
        in_specs=placed,
        out_specs=(P(("dom", "dev"), None), P(("dom", "dev"), None), P()),
        check_vma=False,
    )
```

profile of v0, /device:TPU:8, one launch (start us, length us, event | category | flops | bytes accessed | tf_op | source)
XLA Modules:
  0.0 546.6 jit_solution(14761285722530708981)
XLA Ops:
  7.9 3.8 gather_fusion
  11.7 14.1 %all-to-all-start = ((bf16[64,1,128,256]{3,2,1,0:T(8,128)(2,1)}), bf16[64,1,128,256]{3,2,1,0:T(8,128)(2,1)}, u32[]{:S(2)}, u32[]{:S(2)}) async-start(bf16[64,1,128,256]{3,2,1,0:T(8,128)(2,1)} %bitcast.100), calls=%async_computation | async-start | bytes 8388608 | tf_op jit(solution)/shard_map/all_to_all | solution.py:47
  26.7 17.3 %collective-permute-done = bf16[8,128,256]{2,1,0:T(8,128)(2,1)S(1)} collective-permute-done((bf16[8,128,256]{2,1,0:T(8,128)(2,1)S(1)}, bf16[8,128,256]{2,1,0:T(8,128)(2,1)S(1)}, u32[]{:S(2)}, u32[]{:S(2)}) %collective-permute-start) | collective-permute-done | bytes 524320 | tf_op jit(solution)/shard_map/ppermute | solution.py:12
  44.7 11.0 %collective-permute-done.1 = bf16[8,128,256]{2,1,0:T(8,128)(2,1)} collective-permute-done((bf16[8,128,256]{2,1,0:T(8,128)(2,1)S(1)}, bf16[8,128,256]{2,1,0:T(8,128)(2,1)}, u32[]{:S(2)}, u32[]{:S(2)}) %collective-permute-start.1) | collective-permute-done | bytes 524320 | tf_op jit(solution)/shard_map/ppermute | solution.py:12
  55.7 2.9 convolution_bitcast_fusion.5
  65.0 2.9 copy.38
  75.9 48.2 %all-to-all-done = bf16[64,1,128,256]{3,2,1,0:T(8,128)(2,1)} async-done(((bf16[64,1,128,256]{3,2,1,0:T(8,128)(2,1)}), bf16[64,1,128,256]{3,2,1,0:T(8,128)(2,1)}, u32[]{:S(2)}, u32[]{:S(2)}) %all-to-all-start) | async-done | bytes 4194336 | tf_op jit(solution)/shard_map/all_to_all | solution.py:47
  124.0 4.3 gather_fusion.1
  128.3 4.3 fusion.1
  132.7 6.5 %scatter_fusion = f32[8,128,256]{2,1,0:T(8,128)S(1)} fusion(f32[8,128,256]{2,1,0:T(8,128)S(1)} %broadcast_in_dim.4.clone, s32[32]{0:T(128)S(1)} %fusion.16, f32[32,128,256]{2,1,0:T(8,128)} %fusion.1), kind=kCustom, calls=%fused_computation.9 | custom fusion | flops 1048576 | bytes 12583040 | tf_op jit(solution)/shard_map/scatter-add | solution.py:52
  141.4 3.6 scatter_fusion.2
  151.4 4.3 fusion
  155.7 4.2 broadcast_in_dim.5
  160.0 10.2 %scatter_fusion.7 = f32[64,128,256]{2,1,0:T(8,128)} fusion(f32[64,128,256]{2,1,0:T(8,128)} %broadcast_in_dim.5, s32[32]{0:T(128)S(1)} %fusion.18, f32[32,128,256]{2,1,0:T(8,128)} %fusion), kind=kCustom, calls=%fused_computation.16 | custom fusion | flops 1048576 | bytes 12583040 | tf_op jit(solution)/shard_map/scatter-add | solution.py:87
  170.2 6.2 %all-to-all-start.1 = ((f32[64,1,128,256]{3,2,1,0:T(8,128)}), f32[64,1,128,256]{3,2,1,0:T(8,128)}, u32[]{:S(2)}, u32[]{:S(2)}) async-start(f32[64,1,128,256]{3,2,1,0:T(8,128)} %bitcast.97), calls=%async_computation.1 | async-start | bytes 16777216 | tf_op jit(solution)/shard_map/all_to_all | solution.py:90
  181.8 3.5 scatter_fusion.4
  187.3 3.0 convolution_bitcast_fusion.1
  190.3 2.9 copy.44
  193.3 18.8 %collective-permute-done.3 = f32[8,128,256]{2,1,0:T(8,128)} collective-permute-done((f32[8,128,256]{2,1,0:T(8,128)S(1)}, f32[8,128,256]{2,1,0:T(8,128)}, u32[]{:S(2)}, u32[]{:S(2)}) %collective-permute-start.3) | collective-permute-done | bytes 1048608 | tf_op jit(solution)/shard_map/ppermute | solution.py:12
  212.1 5.0 scatter_fusion.5
  223.9 15.4 %collective-permute-done.4 = f32[8,128,256]{2,1,0:T(8,128)} collective-permute-done((f32[8,128,256]{2,1,0:T(8,128)}, f32[8,128,256]{2,1,0:T(8,128)}, u32[]{:S(2)}, u32[]{:S(2)}) %collective-permute-start.4) | collective-permute-done | bytes 1048608 | tf_op jit(solution)/shard_map/ppermute | solution.py:12
  239.4 4.3 scatter_fusion.6
  247.0 277.8 %all-reduce.2.cloned.1.call-done = f32[256,256]{1,0:T(8,128)} async-done(((f32[256,256]{1,0:T(8,128)}), f32[256,256]{1,0:T(8,128)}) %all-reduce.2.cloned.1.call-update) | async-done | bytes 262160 | tf_op jit(solution)/shard_map/psum | solution.py:75
  526.5 12.4 %scatter_fusion.8 = f32[8,128,256]{2,1,0:T(8,128)S(1)} fusion(f32[8,128,256]{2,1,0:T(8,128)S(1)} %collective-permute-done.5, s32[64]{0:T(128)S(1)} %fusion.17, f32[64,128,256]{2,1,0:T(8,128)} %bitcast.36), kind=kCustom, calls=%fused_computation.17 | custom fusion | flops 2097152 | bytes 25166080 | tf_op jit(solution)/shard_map/scatter-add | solution.py:91
  (78 shorter events, 44.6 us)
Async XLA Ops:
  7.2 140.1 %copy-start = (bf16[256,256]{1,0:T(8,128)(2,1)S(1)}, bf16[256,256]{1,0:T(8,128)(2,1)}, u32[]{:S(2)}) copy-start(bf16[256,256]{1,0:T(8,128)(2,1)} %param.12) | copy-start | bytes 393220
  11.7 14.1 %copy-start.2 = (bf16[1024,256]{1,0:T(8,128)(2,1)S(1)}, bf16[1024,256]{1,0:T(8,128)(2,1)}, u32[]{:S(2)}) copy-start(bf16[1024,256]{1,0:T(8,128)(2,1)} %param.11) | copy-start | bytes 1572868
  11.7 14.9 %copy-start.10 = (s32[1,1,3,16]{3,1,2,0:T(1,128)S(1)}, s32[1,1,3,16]{3,1,2,0:T(1,128)}, u32[]{:S(2)}) copy-start(s32[1,1,3,16]{3,1,2,0:T(1,128)} %param.20) | copy-start | bytes 580
  11.7 14.9 %copy-start.12 = (s32[1,1,32]{2,1,0:T(1,128)S(1)}, s32[1,1,32]{2,1,0:T(1,128)}, u32[]{:S(2)}) copy-start(s32[1,1,32]{2,1,0:T(1,128)} %param.16) | copy-start | bytes 388
  11.7 32.3 %copy-start.13 = (s32[1,1,32]{2,1,0:T(1,128)S(1)}, s32[1,1,32]{2,1,0:T(1,128)}, u32[]{:S(2)}) copy-start(s32[1,1,32]{2,1,0:T(1,128)} %param.15) | copy-start | bytes 388
  11.7 32.3 %copy-start.11 = (s32[1,1,3,16]{3,1,2,0:T(1,128)S(1)}, s32[1,1,3,16]{3,1,2,0:T(1,128)}, u32[]{:S(2)}) copy-start(s32[1,1,3,16]{3,1,2,0:T(1,128)} %param.19) | copy-start | bytes 580
  11.7 112.3 %all-to-all-start = ((bf16[64,1,128,256]{3,2,1,0:T(8,128)(2,1)}), bf16[64,1,128,256]{3,2,1,0:T(8,128)(2,1)}, u32[]{:S(2)}, u32[]{:S(2)}) async-start(bf16[64,1,128,256]{3,2,1,0:T(8,128)(2,1)} %bitcast.100), calls=%async_computation | async-start | bytes 8388608 | tf_op jit(solution)/shard_map/all_to_all | solution.py:47
  25.8 18.2 %collective-permute-start = (bf16[8,128,256]{2,1,0:T(8,128)(2,1)S(1)}, bf16[8,128,256]{2,1,0:T(8,128)(2,1)S(1)}, u32[]{:S(2)}, u32[]{:S(2)}) collective-permute-start(bf16[8,128,256]{2,1,0:T(8,128)(2,1)S(1)} %bitcast.99), channel_id=1, source_target_pairs={{0,64},{64,128},{128,192},{192,0},{1,65},{65,129},{129,193},{193,1... | collective-permute-start | bytes 1572872 | tf_op jit(solution)/shard_map/ppermute | solution.py:12
  44.0 11.7 %collective-permute-start.1 = (bf16[8,128,256]{2,1,0:T(8,128)(2,1)S(1)}, bf16[8,128,256]{2,1,0:T(8,128)(2,1)}, u32[]{:S(2)}, u32[]{:S(2)}) collective-permute-start(bf16[8,128,256]{2,1,0:T(8,128)(2,1)S(1)} %collective-permute-done), channel_id=1, source_target_pairs={{0,64},{64,128},{128,192},{192,0},{1,65},{65,129},{129,193},{193,1... | collective-permute-start | bytes 1572872 | tf_op jit(solution)/shard_map/ppermute | solution.py:12
  55.7 12.8 %collective-permute-start.2 = (bf16[8,128,256]{2,1,0:T(8,128)(2,1)}, bf16[8,128,256]{2,1,0:T(8,128)(2,1)}, u32[]{:S(2)}, u32[]{:S(2)}) collective-permute-start(bf16[8,128,256]{2,1,0:T(8,128)(2,1)} %collective-permute-done.1), channel_id=1, source_target_pairs={{0,64},{64,128},{128,192},{192,0},{1,65},{65,129},{129,193},{193,1... | collective-permute-start | bytes 1572872 | tf_op jit(solution)/shard_map/ppermute | solution.py:12
  124.0 4.3 copy-start.5
  141.4 3.6 copy-start.3
  147.2 2.7 copy-start.6
  149.9 0.8 copy-start.8
  170.2 356.3 %all-to-all-start.1 = ((f32[64,1,128,256]{3,2,1,0:T(8,128)}), f32[64,1,128,256]{3,2,1,0:T(8,128)}, u32[]{:S(2)}, u32[]{:S(2)}) async-start(f32[64,1,128,256]{3,2,1,0:T(8,128)} %bitcast.97), calls=%async_computation.1 | async-start | bytes 16777216 | tf_op jit(solution)/shard_map/all_to_all | solution.py:90
  176.4 348.4 %all-reduce.2.cloned.1.call-start = ((), (), s32[]{:S(2)}) async-start(), calls=%async_computation.2 | async-start | bytes 524288 | tf_op jit(solution)/shard_map/psum | solution.py:75
  185.3 2.0 copy-start.4
  185.3 26.8 %collective-permute-start.3 = (f32[8,128,256]{2,1,0:T(8,128)S(1)}, f32[8,128,256]{2,1,0:T(8,128)}, u32[]{:S(2)}, u32[]{:S(2)}) collective-permute-start(f32[8,128,256]{2,1,0:T(8,128)S(1)} %scatter_fusion.4), channel_id=1, source_target_pairs={{0,192},{64,0},{128,64},{192,128},{1,193},{65,1},{129,65},{193,129... | collective-permute-start | bytes 3145736 | tf_op jit(solution)/shard_map/ppermute | solution.py:12
  217.1 22.3 %collective-permute-start.4 = (f32[8,128,256]{2,1,0:T(8,128)}, f32[8,128,256]{2,1,0:T(8,128)}, u32[]{:S(2)}, u32[]{:S(2)}) collective-permute-start(f32[8,128,256]{2,1,0:T(8,128)} %scatter_fusion.5), channel_id=1, source_target_pairs={{0,192},{64,0},{128,64},{192,128},{1,193},{65,1},{129,65},{193,129... | collective-permute-start | bytes 3145736 | tf_op jit(solution)/shard_map/ppermute | solution.py:12
  223.9 22.1 %copy-start.7 = (bf16[8,128,256]{2,1,0:T(8,128)(2,1)S(1)}, bf16[8,128,256]{2,1,0:T(8,128)(2,1)}, u32[]{:S(2)}) copy-start(bf16[8,128,256]{2,1,0:T(8,128)(2,1)} %copy-done.6) | copy-start | bytes 1572868
  223.9 22.0 %copy-start.9 = (bf16[1024,256]{1,0:T(8,128)(2,1)S(1)}, bf16[1024,256]{1,0:T(8,128)(2,1)}, u32[]{:S(2)}) copy-start(bf16[1024,256]{1,0:T(8,128)(2,1)} %copy-done.8) | copy-start | bytes 1572868
  243.6 282.8 %collective-permute-start.5 = (f32[8,128,256]{2,1,0:T(8,128)}, f32[8,128,256]{2,1,0:T(8,128)S(1)}, u32[]{:S(2)}, u32[]{:S(2)}) collective-permute-start(f32[8,128,256]{2,1,0:T(8,128)} %scatter_fusion.6), channel_id=1, source_target_pairs={{0,192},{64,0},{128,64},{192,128},{1,193},{65,1},{129,65},{193,129... | collective-permute-start | bytes 3145736 | tf_op jit(solution)/shard_map/ppermute | solution.py:12
  526.5 13.2 %copy-start.1 = (bf16[256,256]{1,0:T(8,128)(2,1)S(1)}, bf16[256,256]{1,0:T(8,128)(2,1)}, u32[]{:S(2)}) copy-start(bf16[256,256]{1,0:T(8,128)(2,1)} %param.12) | copy-start | bytes 393220
Sparse Core Ops, SparseCore 0:
  247.1 277.6 all-reduce.1
where the time goes:
time: 548 us; the launch traced here: 547 us
  waiting for transfers between devices  389 us (71%)
  other arithmetic  53.1 us (10%)
  local copies, waits for them, and re-layouts  35.9 us (7%)
  matrix products  27.9 us (5%)
  starting transfers between devices  25.6 us (5%)
  between operations  15.1 us (3%)
    psum x1, waiting for transfers between devices, body(): weight_sum_all = lax.psum(partial_weight, ('dom', 'dev'))  278 us
    ppermute x6, waiting for transfers between devices, from_behind(): return lax.ppermute(value, axis, pairs)  63.1 us
    all_to_all x1, waiting for transfers between devices, body(): lax.all_to_all(outgoing, 'dev', split_axis=0, concat_axis=0, tiled=True)  48.2 us
    all_to_all x1, starting transfers between devices, body(): lax.all_to_all(outgoing, 'dev', split_axis=0, concat_axis=0, tiled=True)  14.1 us
    scatter-add x3, other arithmetic, body(): zero_blocks.at[cross_col[group]].add(cross_out)  12.7 us
    scatter-add x1, other arithmetic, body(): zero_blocks.at[flat_slots]  12.4 us
  transfers between devices with their start and end apart: 9, of which 7 were waited for; matrix products, arithmetic and copies ran while one was open for 10% of the time, Pallas kernels for 0%

commit v1 on v0

v1 whole, which is shorter than its diff:
```python
import functools
import math

import jax
import jax.numpy as jnp
from jax import lax
from jax.experimental import pallas as pl
from jax.experimental.pallas import tpu as pltpu
from jax.sharding import PartitionSpec as P

MESH = pl.DeviceIdType.MESH
BF = jnp.bfloat16
F32 = jnp.float32
NX, NY, NZ = 4, 2, 8
RB, BLK, F = 8, 128, 256
N_DOM = 4
KIN, KX = 32, 16
HALF = RB // 2
RELS = (0, -1, 1, -2, 2, -3, 3, 4)
SLOT = {rel: i for i, rel in enumerate(RELS)}


def position():
    dom = lax.axis_index("dom")
    dev = lax.axis_index("dev")
    return dom, dev, dev // 16, (dev // 8) % 2, dev % 8


def dev_of(x, yh, z):
    return x * 16 + yh * 8 + z


def remote(src, dst, send_sem, recv_sem, dom, dev):
    return pltpu.make_async_remote_copy(
        src_ref=src, dst_ref=dst, send_sem=send_sem, recv_sem=recv_sem,
        device_id=(dom, dev), device_id_type=MESH)


def greet(peers):
    barrier = pltpu.get_barrier_semaphore()
    for dom, dev in peers:
        pl.semaphore_signal(barrier, inc=1, device_id=(dom, dev), device_id_type=MESH)
    pl.semaphore_wait(barrier, len(peers))


def gather_kernel(feat, slots_sm, slots_vm, pool, rem, tab,
                  b1, b2, b3, b4, b5, b6, b7, stage, relay, tab_vm, tab_sm,
                  meta_s, meta_r, zs, zr, xs, xr, ys, yr, ls, ds, dr, ts):
    dom, dev, x, yh, z = position()
    yo = 1 - yh
    bufs = dict(zip(RELS, (feat, b1, b2, b3, b4, b5, b6, b7)))

    def zdev(rel):
        return dev_of(x, yh, (z + rel + NZ) % NZ)

    def xdev(dx):
        return dev_of((x + dx) % NX, yh, z)

    ydev = dev_of(x, yo, z)
    sib = dom + 1 - 2 * (dom % 2)
    far = (dom + 2) % N_DOM

    greet([(dom, zdev(rel)) for rel in RELS[1:]] + [(dom, xdev(dx)) for dx in (1, 2, 3)]
          + [(dom, ydev), (sib, dev), (far, dev)])

    live = []

    def go(copy):
        copy.start()
        live.append(copy)
        return copy

    for rel in RELS[1:]:
        i = SLOT[-rel] if rel != 4 else SLOT[4]
        go(remote(slots_vm, tab_vm.at[i], meta_s.at[i], meta_r.at[i], dom, zdev(rel)))

    def zcopy(src_rel, dst_rel, piece, step):
        part = pl.ds(piece * HALF, HALF)
        s = SLOT[dst_rel] * 2 + piece
        return remote(bufs[src_rel].at[part], bufs[dst_rel].at[part], zs.at[s], zr.at[s], dom, zdev(step))

    for n in (0, 1):
        go(zcopy(0, -1, n, 1))
        go(zcopy(0, 1, 1 - n, -1))
    o_sib = (sib - dom - 1 + 2 * N_DOM) % N_DOM
    go(remote(feat, rem.at[o_sib], ds.at[0], dr.at[0], sib, dev))
    go(remote(feat, rem.at[1], ds.at[1], dr.at[1], far, dev))

    def serve(rel):
        i = SLOT[rel]
        buf = bufs[rel]
        zsrc = (z + rel + NZ) % NZ
        for xx in range(NX):
            for g, y in ((0, yo), (1, yh)):
                where = dev_of(xx, y, z)
                if rel == 0:
                    pick = slots_sm[where]
                else:
                    pick = tab_sm[i, 0, where]
                stage[i, g, xx] = buf[pick]
        go(remote(stage.at[i, 0], relay.at[i], ys.at[i], yr.at[i], dom, ydev))
        for dx in (1, 2, 3):
            go(remote(stage.at[i, 1, (x + dx) % NX], pool.at[dev_of(x, yh, zsrc)],
                      xs.at[i, 0, dx], xr.at[i, 0, dx], dom, xdev(dx)))
        go(pltpu.make_async_copy(stage.at[i, 1, x], pool.at[dev_of(x, yh, zsrc)], ls.at[i, 0]))

    def pass_on(rel):
        i = SLOT[rel]
        zsrc = (z + rel + NZ) % NZ
        remote(stage.at[i, 0], relay.at[i], ys.at[i], yr.at[i], dom, ydev).wait_recv()
        for dx in (1, 2, 3):
            go(remote(relay.at[i, (x + dx) % NX], pool.at[dev_of(x, yo, zsrc)],
                      xs.at[i, 1, dx], xr.at[i, 1, dx], dom, xdev(dx)))
        go(pltpu.make_async_copy(relay.at[i, x], pool.at[dev_of(x, yo, zsrc)], ls.at[i, 1]))

    serve(0)
    for rel in RELS[1:]:
        i = SLOT[rel]
        remote(slots_vm, tab_vm.at[i], meta_s.at[i], meta_r.at[i], dom, zdev(rel)).wait_recv()
    tab_vm[0] = slots_vm[...]
    to_sm = pltpu.make_async_copy(tab_vm, tab_sm, ts.at[0])
    to_sm.start()
    to_out = pltpu.make_async_copy(tab_vm, tab, ts.at[1])
    to_out.start()
    to_sm.wait()

    for j in (1, 2, 3):
        for n in (0, 1):
            zcopy(0, -j, n, 1).wait_recv()
            if j < 3:
                go(zcopy(-j, -j - 1, n, 1))
            elif n == 0:
                go(zcopy(-3, 4, 0, 1))
            zcopy(0, j, 1 - n, -1).wait_recv()
            if j < 3:
                go(zcopy(j, j + 1, 1 - n, -1))
            elif n == 0:
                go(zcopy(3, 4, 1, -1))
        serve(-j)
        serve(j)
        if j == 1:
            pass_on(0)
            remote(feat, rem.at[1], ds.at[1], dr.at[1], far, dev).wait_recv()
            o_far = (sib - far - 1 + 2 * N_DOM) % N_DOM
            go(remote(rem.at[1], rem.at[o_far], ds.at[2], dr.at[2], sib, dev))
        else:
            pass_on(1 - j)
            pass_on(j - 1)
    zcopy(0, 4, 0, 1).wait_recv()
    zcopy(0, 4, 1, -1).wait_recv()
    serve(4)
    pass_on(-3)
    pass_on(3)
    pass_on(4)

    remote(feat, rem.at[o_sib], ds.at[0], dr.at[0], sib, dev).wait_recv()
    remote(feat, rem.at[o_sib], ds.at[2], dr.at[2], sib, dev).wait_recv()
    for rel in RELS:
        i = SLOT[rel]
        for g in (0, 1):
            for dx in (1, 2, 3):
                remote(relay.at[0, 0], pool.at[0], xs.at[i, g, dx], xr.at[i, g, dx], dom, xdev(dx)).wait_recv()
    for copy in live:
        if hasattr(copy, "wait_send") and copy.is_remote:
            copy.wait_send()
        else:
            copy.wait()
    to_out.wait()


def gather(features, send_row):
    vm = pl.BlockSpec(memory_space=pltpu.VMEM)
    sm = pl.BlockSpec(memory_space=pltpu.SMEM)
    hbm = pl.BlockSpec(memory_space=pl.ANY)
    dma = pltpu.SemaphoreType.DMA
    padded = jnp.zeros((8, 128), jnp.int32).at[0, : send_row.shape[0]].set(send_row)
    return pl.pallas_call(
        gather_kernel,
        out_shape=(
            jax.ShapeDtypeStruct((NX * NY * NZ, BLK, F), BF),
            jax.ShapeDtypeStruct((N_DOM - 1, RB, BLK, F), BF),
            jax.ShapeDtypeStruct((NZ, 8, 128), jnp.int32),
        ),
        in_specs=[vm, sm, vm],
        out_specs=(hbm, hbm, hbm),
        scratch_shapes=[pltpu.VMEM((RB, BLK, F), BF)] * 7 + [
            pltpu.VMEM((NZ, 2, NX, BLK, F), BF),
            pltpu.VMEM((NZ, NX, BLK, F), BF),
            pltpu.VMEM((NZ, 8, 128), jnp.int32),
            pltpu.SMEM((NZ, 8, 128), jnp.int32),
            dma((NZ,)), dma((NZ,)),
            dma((2 * NZ,)), dma((2 * NZ,)),
            dma((NZ, 2, 4)), dma((NZ, 2, 4)),
            dma((NZ,)), dma((NZ,)),
            dma((NZ, 2)),
            dma((3,)), dma((3,)),
            dma((2,)),
        ],
        compiler_params=pltpu.CompilerParams(
            collective_id=0, has_side_effects=True, vmem_limit_bytes=40 << 20),
        name="gather_blocks",
    )(features, send_row, padded)


def layer_kernel(rows_sm, src_sm, count_sm, crow_sm, ccol_sm, pool, rem, ivals, cvals, w, cot,
                 act, sums, csums, wpart, acc, back, slots, cacc):
    count = count_sm[0, 0]
    acc[...] = jnp.zeros_like(acc)

    for o in range(N_DOM - 1):
        def cross(k4, carry, o=o):
            for u in range(4):
                k = k4 * 4 + u
                acc[crow_sm[0, 0, o, k]] += jnp.dot(
                    cvals[o, k], rem[o, ccol_sm[0, 0, o, k]], preferred_element_type=F32)
            return carry
        lax.fori_loop(0, KX // 4, cross, 0)

    def intra(k4, carry):
        for u in range(4):
            k = k4 * 4 + u
            part = jnp.dot(ivals[k], pool[src_sm[0, 0, k]], preferred_element_type=F32)
            acc[rows_sm[0, 0, k]] += jnp.where(k < count, part, 0.0)
        return carry
    lax.fori_loop(0, (count + 3) // 4, intra, 0)

    wpart[...] = jnp.zeros_like(wpart)

    def dense(r, carry):
        agg = acc[r].astype(BF)
        pre = jnp.dot(agg, w[...], preferred_element_type=F32)
        sig = jax.nn.sigmoid(pre)
        act[r] = (pre * sig).astype(BF)
        grad = (cot[r].astype(F32) * sig * (1.0 + pre * (1.0 - sig))).astype(BF)
        wpart[...] += lax.dot_general(agg, grad, (((0,), (0,)), ((), ())), preferred_element_type=F32)
        back[r] = lax.dot_general(
            grad, w[...], (((1,), (1,)), ((), ())), preferred_element_type=F32).astype(BF)
        return carry
    lax.fori_loop(0, RB, dense, 0)

    slots[...] = jnp.zeros_like(slots)
    cacc[...] = jnp.zeros_like(cacc)
    turned = (((0,), (0,)), ((), ()))

    def intra_back(k4, carry):
        for u in range(4):
            k = k4 * 4 + u
            part = lax.dot_general(ivals[k], back[rows_sm[0, 0, k]], turned, preferred_element_type=F32)
            slots[src_sm[0, 0, k]] += jnp.where(k < count, part, 0.0)
        return carry
    lax.fori_loop(0, (count + 3) // 4, intra_back, 0)

    for o in range(N_DOM - 1):
        def cross_back(k4, carry, o=o):
            for u in range(4):
                k = k4 * 4 + u
                cacc[o, ccol_sm[0, 0, o, k]] += lax.dot_general(
                    cvals[o, k], back[crow_sm[0, 0, o, k]], turned, preferred_element_type=F32)
            return carry
        lax.fori_loop(0, KX // 4, cross_back, 0)

    def narrow(i, carry):
        sums[i] = slots[i].astype(BF)
        return carry
    lax.fori_loop(0, NX * NY * NZ, narrow, 0)
    for o in range(N_DOM - 1):
        for b in range(RB):
            csums[o, b] = cacc[o, b].astype(BF)


def layer(rows, src, count, crow, ccol, pool, rem, ivals, cvals, w, cot):
    vm = pl.BlockSpec(memory_space=pltpu.VMEM)
    sm = pl.BlockSpec(memory_space=pltpu.SMEM)
    n = NX * NY * NZ
    return pl.pallas_call(
        layer_kernel,
        out_shape=(
            jax.ShapeDtypeStruct((RB, BLK, F), BF),
            jax.ShapeDtypeStruct((n, BLK, F), BF),
            jax.ShapeDtypeStruct((N_DOM - 1, RB, BLK, F), BF),
            jax.ShapeDtypeStruct((F, F), F32),
        ),
        in_specs=[sm] * 5 + [vm] * 6,
        out_specs=(vm, vm, vm, vm),
        scratch_shapes=[
            pltpu.VMEM((RB, BLK, F), F32),
            pltpu.VMEM((RB, BLK, F), BF),
            pltpu.VMEM((n, BLK, F), F32),
            pltpu.VMEM((N_DOM - 1, RB, BLK, F), F32),
        ],
        compiler_params=pltpu.CompilerParams(vmem_limit_bytes=56 << 20),
        name="layer_tiles",
    )(rows, src, count, crow, ccol, pool, rem, ivals, cvals, w, cot)


BACK_RELS = (4, 3, -3, 2, -2, 1, -1, 0)
STRIP = 16
W_SCALE = 1.0 / math.sqrt(RB * BLK * NX * NY * NZ * N_DOM)


def scatter_kernel(sums, csums, tab, wpart, out, wg,
                   xbuf, ybuf, part, rin, lin, near, far_in, pair, far_got, wquarter, wplane, wline,
                   xs, xr, ls, ys, yr, rs, rr, lts, ltr, ds, dr, ws, wr):
    dom, dev, x, yh, z = position()
    yo = 1 - yh
    place = x * NY + yh

    def zdev(rel):
        return dev_of(x, yh, (z + rel + NZ) % NZ)

    def xdev(dx):
        return dev_of((x + dx) % NX, yh, z)

    ydev = dev_of(x, yo, z)
    sib = dom + 1 - 2 * (dom % 2)
    far = (dom + 2) % N_DOM
    sib_far = (sib + 2) % N_DOM

    def o_of(target):
        return (dom - target - 1 + 2 * N_DOM) % N_DOM

    plane = [(dx, dy) for dy in (0, 1) for dx in range(NX) if dx or dy]

    def pdev(dx, dy):
        return dev_of((x + dx) % NX, (yh + dy) % NY, z)

    greet([(dom, zdev(rel)) for rel in RELS[1:]] + [(dom, pdev(dx, dy)) for dx, dy in plane]
          + [(sib, dev), (far, dev), (sib_far, dev)])

    live = []

    def go(copy):
        copy.start()
        live.append(copy)
        return copy

    doms = (sib, far, sib_far)
    wrows = F // N_DOM
    first = dom * wrows + place * 8

    def w_dom(n):
        return remote(wpart.at[pl.ds(doms[n] * wrows, wrows)], wquarter.at[n], ws.at[n], wr.at[n], doms[n], dev)

    def w_plane(n):
        dx, dy = plane[n]
        there = ((x + dx) % NX) * NY + (yh + dy) % NY
        return remote(wquarter.at[3, pl.ds(there * 8, 8)], wplane.at[n], ws.at[3 + n], wr.at[3 + n],
                      dom, pdev(dx, dy))

    def w_line(n):
        return remote(wplane.at[7], wline.at[z], ws.at[10 + n], wr.at[10 + n], dom, zdev(RELS[1 + n]))

    def w_plane_back(n):
        dx, dy = plane[n]
        rows = pl.ds(first, 8)
        return remote(wg.at[rows], wg.at[rows], ws.at[17 + n], wr.at[17 + n], dom, pdev(dx, dy))

    def w_dom_back(n):
        rows = pl.ds(dom * wrows, wrows)
        return remote(wg.at[rows], wg.at[rows], ws.at[24 + n], wr.at[24 + n], doms[n], dev)

    def w_step(step):
        if step == 0:
            for n in range(3):
                go(w_dom(n))
        if step == 1:
            for n in range(3):
                w_dom(n).wait_recv()
            wquarter[3] = (wpart[pl.ds(dom * wrows, wrows)] + wquarter[0]) + (wquarter[1] + wquarter[2])
            for n in range(7):
                go(w_plane(n))
        if step == 2:
            for n in range(7):
                w_plane(n).wait_recv()
            total = wquarter[3, pl.ds(place * 8, 8)]
            for n in range(7):
                total = total + wplane[n]
            wplane[7] = total
            wline[z] = total
            for n in range(7):
                go(w_line(n))
        if step == 3:
            for n in range(7):
                w_line(n).wait_recv()
            total = wline[0]
            for n in range(1, NZ):
                total = total + wline[n]
            wg[pl.ds(first, 8)] = total * W_SCALE
            for n in range(7):
                go(w_plane_back(n))
        if step == 4:
            for n in range(7):
                w_plane_back(n).wait_recv()
            for n in range(3):
                go(w_dom_back(n))
        if step == 5:
            for n in range(3):
                w_dom_back(n).wait_recv()

    go(remote(csums.at[o_of(sib_far)], pair, ds.at[0], dr.at[0], sib, dev))
    go(remote(csums.at[o_of(sib)], near, ds.at[1], dr.at[1], sib, dev))

    def xsend(rel):
        i = SLOT[rel]
        zdst = (z + rel + NZ) % NZ
        for dx in (1, 2, 3):
            go(remote(sums.at[(x + dx) % NX, :, zdst], xbuf.at[i, dx], xs.at[i, dx], xr.at[i, dx],
                      dom, xdev(dx)))
        own = pltpu.make_async_copy(sums.at[x, :, zdst], xbuf.at[i, 0], ls.at[i])
        own.start()

    def ysend(rel):
        i = SLOT[rel]
        zdst = (z + rel + NZ) % NZ
        for dx in (1, 2, 3):
            remote(sums.at[0, :, 0], xbuf.at[i, dx], xs.at[i, dx], xr.at[i, dx], dom, xdev(dx)).wait_recv()
        pltpu.make_async_copy(sums.at[x, :, zdst], xbuf.at[i, 0], ls.at[i]).wait()
        go(remote(xbuf.at[i, :, yo], ybuf.at[i], ys.at[i], yr.at[i], dom, ydev))

    def ywait(rel):
        i = SLOT[rel]
        remote(xbuf.at[i, :, yo], ybuf.at[i], ys.at[i], yr.at[i], dom, ydev).wait_recv()

    def combine(rel, extra, store):
        i = SLOT[rel]
        picks = []
        for g, y in ((0, yh), (1, yo)):
            for dx in range(NX):
                d = dev_of((x - dx + NX) % NX, y, z)
                pick = tab[i, 0, d]
                picks.append((g, dx, [jnp.where(pick == b, 1.0, 0.0).astype(F32) for b in range(RB)]))

        def strip(s, carry):
            rows = pl.ds(pl.multiple_of(s * STRIP, STRIP), STRIP)
            totals = [None] * RB
            for g, dx, on in picks:
                got = (xbuf[i, dx, yh, rows] if g == 0 else ybuf[i, dx, rows]).astype(F32)
                for b in range(RB):
                    term = got * on[b]
                    totals[b] = term if totals[b] is None else totals[b] + term
            for b in range(RB):
                total = totals[b]
                for ref, blocks in extra:
                    if b in blocks:
                        total = total + ref[b, rows].astype(F32)
                store[b, rows] = total.astype(BF)
            return carry
        lax.fori_loop(0, BLK // STRIP, strip, 0)

    every = tuple(range(RB))
    low, high = every[:HALF], every[HALF:]

    def rcopy(src_rel, j):
        i = SLOT[src_rel]
        if j == 3:
            a = pl.ds(0, HALF)
            return remote(part.at[i, a], rin.at[j, a], rs.at[j], rr.at[j], dom, zdev(1))
        return remote(part.at[i], rin.at[j], rs.at[j], rr.at[j], dom, zdev(1))

    def lcopy(src_rel, j):
        i = SLOT[src_rel]
        if j == 3:
            a = pl.ds(HALF, HALF)
            return remote(part.at[i, a], lin.at[j, a], lts.at[j], ltr.at[j], dom, zdev(-1))
        return remote(part.at[i], lin.at[j], lts.at[j], ltr.at[j], dom, zdev(-1))

    w_step(0)
    xsend(4)
    xsend(3)
    xsend(-3)
    remote(csums.at[0], pair, ds.at[0], dr.at[0], sib, dev).wait_recv()

    def add_pair(b, carry):
        far_in[b] = (pair[b].astype(F32) + csums[o_of(far), b].astype(F32)).astype(BF)
        return carry
    lax.fori_loop(0, RB, add_pair, 0)
    w_step(1)
    ysend(4)
    xsend(2)
    xsend(-2)
    ysend(3)
    ysend(-3)
    go(remote(far_in, far_got, ds.at[2], dr.at[2], far, dev))
    ywait(4)
    combine(4, [], part.at[SLOT[4]])
    go(rcopy(4, 3))
    go(lcopy(4, 3))
    w_step(2)
    for j in (3, 2, 1):
        if j == 3:
            xsend(1)
            xsend(-1)
        if j == 2:
            xsend(0)
        if j > 1:
            ysend(j - 1)
            ysend(1 - j)
        else:
            ysend(0)
        ywait(j)
        rcopy(4, j).wait_recv()
        combine(j, [(rin.at[j], low if j == 3 else every)], part.at[SLOT[j]])
        go(rcopy(j, j - 1))
        ywait(-j)
        lcopy(4, j).wait_recv()
        combine(-j, [(lin.at[j], high if j == 3 else every)], part.at[SLOT[-j]])
        go(lcopy(-j, j - 1))
        w_step(6 - j)
    ywait(0)
    remote(csums.at[0], near, ds.at[1], dr.at[1], sib, dev).wait_recv()
    remote(far_in, far_got, ds.at[2], dr.at[2], far, dev).wait_recv()
    rcopy(4, 0).wait_recv()
    lcopy(4, 0).wait_recv()
    combine(0, [(rin.at[0], every), (lin.at[0], every), (near, every), (far_got, every)], out)
    for copy in live:
        copy.wait_send()


def scatter(sums, csums, tab, wpart):
    vm = pl.BlockSpec(memory_space=pltpu.VMEM)
    sm = pl.BlockSpec(memory_space=pltpu.SMEM)
    dma = pltpu.SemaphoreType.DMA
    block = (RB, BLK, F)
    return pl.pallas_call(
        scatter_kernel,
        out_shape=(jax.ShapeDtypeStruct(block, BF), jax.ShapeDtypeStruct((F, F), F32)),
        in_specs=[vm, vm, sm, vm],
        out_specs=(vm, vm),
        scratch_shapes=[
            pltpu.VMEM((NZ, NX, NY, BLK, F), BF),
            pltpu.VMEM((NZ, NX, BLK, F), BF),
            pltpu.VMEM((NZ,) + block, BF),
            pltpu.VMEM((4,) + block, BF),
            pltpu.VMEM((4,) + block, BF),
            pltpu.VMEM(block, BF), pltpu.VMEM(block, BF), pltpu.VMEM(block, BF), pltpu.VMEM(block, BF),
            pltpu.VMEM((4, F // N_DOM, F), F32), pltpu.VMEM((8, 8, F), F32), pltpu.VMEM((NZ, 8, F), F32),
            dma((NZ, 4)), dma((NZ, 4)), dma((NZ,)),
            dma((NZ,)), dma((NZ,)),
            dma((4,)), dma((4,)), dma((4,)), dma((4,)),
            dma((3,)), dma((3,)),
            dma((27,)), dma((27,)),
        ],
        compiler_params=pltpu.CompilerParams(
            collective_id=1, has_side_effects=True, vmem_limit_bytes=48 << 20),
        name="scatter_sums",
    )(sums.reshape(NX, NY, NZ, BLK, F), csums, tab, wpart)


def body(features, weight, cotangent, send_list, intra_rows, intra_src, intra_count, intra_vals,
         cross_rows, cross_cols, cross_vals):
    own = features.reshape(RB, BLK, F)
    pool, rem, tab = gather(own, send_list.reshape(-1))
    act, sums, csums, wpart = layer(
        intra_rows, intra_src, intra_count, cross_rows, cross_cols, pool, rem,
        intra_vals[0, 0], cross_vals[0, 0], weight, cotangent.reshape(RB, BLK, F))
    input_grad, weight_grad = scatter(sums, csums, tab, wpart)
    return act.reshape(RB * BLK, F), input_grad.reshape(RB * BLK, F), weight_grad


def solution(mesh):
    placed = (
        P(("dom", "dev"), None),
        P(),
        P(("dom", "dev"), None),
        P("dom", "dev", None, None),
        P("dom", "dev", None),
        P("dom", "dev", None),
        P("dom", "dev"),
        P("dom", "dev", None, None, None),
        P("dom", "dev", None, None),
        P("dom", "dev", None, None),
        P("dom", "dev", None, None, None, None),
    )
    return jax.shard_map(
        body,
        mesh=mesh,
        in_specs=placed,
        out_specs=(P(("dom", "dev"), None), P(("dom", "dev"), None), P()),
        check_vma=False,
    )
```

time: 548 us -> 191 us (0.35)
  waiting for transfers between devices: 389 us -> 0 us
  Pallas kernels: 0 us -> 175 us
  other arithmetic: 53.1 us -> 0 us
  matrix products: 27.9 us -> 0 us
  starting transfers between devices: 25.6 us -> 0 us
  local copies, waits for them, and re-layouts: 35.9 us -> 11.9 us
  between operations: 15.1 us -> 1.31 us
    psum x1 -> x0, waiting for transfers between devices: 278 us -> none  [body(): weight_sum_all = lax.psum(partial_weight, ('dom', 'dev'))]
    pallas_call x0 -> x3, Pallas kernels: none -> 175 us  [the longest x1 82 us: scatter(): pl.pallas_call(scatter_kernel, out_shape=(jax.ShapeDtypeStruct(block, BF)...]
    ppermute x6 -> x0, waiting for transfers between devices: 63.1 us -> none  [from_behind(): return lax.ppermute(value, axis, pairs)]
    scatter-add x9 -> x0, other arithmetic: 49.7 us -> none  [the longest x3 12.7 us: body(): zero_blocks.at[cross_col[group]].add(cross_out)]
    all_to_all x2 -> x0, waiting for transfers between devices: 48.2 us -> none  [the longest x1 48.2 us: body(): lax.all_to_all(outgoing, 'dev', split_axis=0, concat_axis=0, tiled=True)]
    dot_general x11 -> x0, matrix products: 27.9 us -> none  [the longest x3 8.6 us: body(): jnp.einsum('kab,kbf->kaf', cross_val[cross_group], remote[cross_col[cross...]
    all_to_all x2 -> x0, starting transfers between devices: 20.3 us -> none  [the longest x1 14.1 us: body(): lax.all_to_all(outgoing, 'dev', split_axis=0, concat_axis=0, tiled=True)]
    gather x9 -> x0, local copies, waits for them, and re-layouts: 16.5 us -> none  [the longest x1 4.28 us: body(): slot_pool[tile_source]]
  transfers between devices with their start and end apart: 9 -> 0, of which waited for: 7 -> 0; matrix products, arithmetic and copies ran while one was open for 10% -> 0% of each run, Pallas kernels for 0% -> 0%
where the time goes in v1:
time: 191 us; the launch traced here: 188 us
  Pallas kernels  175 us (92%)
  local copies, waits for them, and re-layouts  11.9 us (6%)
    pallas_call x1, Pallas kernels, scatter(): pl.pallas_call(scatter_kernel, out_shape=(jax.ShapeDtypeStruct(block, BF)...  82 us
    pallas_call x1, Pallas kernels, gather(): pl.pallas_call(gather_kernel, out_shape=(jax.ShapeDtypeStruct((NX * NY *...  74.8 us
    pallas_call x1, Pallas kernels, layer(): pl.pallas_call(layer_kernel, out_shape=(jax.ShapeDtypeStruct((RB, BLK, F)...  17.9 us
    unnamed x16, local copies, waits for them, and re-layouts  11.2 us

profile of v1, /device:TPU:8, one launch (start us, length us, event | category | flops | bytes accessed | tf_op | source)
XLA Modules:
  0.0 187.8 jit_solution(6206287907278658259)
XLA Ops:
  1.3 1.3 copy.14.crow_sm
  2.5 1.3 copy.15.ccol_sm
  3.8 0.7 scatter.4.slots_vm
  4.5 0.0 copy-start.3
  4.5 1.0 copy-done.3
  5.5 0.0 copy-start.5
  5.5 0.7 copy-done.5
  6.2 74.8 %gather_blocks.1 = (bf16[64,128,256]{2,1,0:T(8,128)(2,1)S(1)}, bf16[3,8,128,256]{3,2,1,0:T(8,128)(2,1)S(1)}, s32[8,8,128]{2,1,0:T(8,128)S(1)}) custom-call(bf16[8,128,256]{2,1,0:T(8,128)(2,1)S(1)} %bitcast.9, s32[64]{0:T(128)S(1)} %bitcast.12, s32[8,128]{1,0:T(8,128)S(1)} %scatter.4.slots_vm), custom_call_target="tpu_custom_call" | custom-call | tf_op jit(solution)/shard_map/gather_blocks/pallas_call | solution.py:177
  80.9 0.0 copy-start
  81.0 1.9 %copy-done = bf16[64,128,256]{2,1,0:T(8,128)(2,1)} copy-done((bf16[64,128,256]{2,1,0:T(8,128)(2,1)}, bf16[64,128,256]{2,1,0:T(8,128)(2,1)S(1)}, u32[]{:S(2)}) %copy-start) | copy-done | bytes 4194328
  82.9 0.0 copy-start.1
  82.9 1.2 copy-done.1
  84.1 17.9 %layer_tiles.1 = (bf16[8,128,256]{2,1,0:T(8,128)(2,1)}, bf16[64,128,256]{2,1,0:T(8,128)(2,1)}, bf16[3,8,128,256]{3,2,1,0:T(8,128)(2,1)}, f32[256,256]{1,0:T(8,128)}) custom-call(s32[1,1,32]{2,1,0:T(1,128)} %rows_sm.1, s32[1,1,32]{2,1,0:T(1,128)} %src_sm.1, s32[1,1]{1,0:T(1,128)S(6)} %copy.18.count_sm, s32[1,1,3,16]{3,2,1,0:T(4,128)} %copy.14.crow_sm, ...), custom_call_target="tpu_custom_call" | custom-call | tf_op jit(solution)/shard_map/layer_tiles/pallas_call | solution.py:275
  102.0 0.0 copy-start.2
  102.0 1.4 copy-done.2
  103.4 0.0 copy-start.4
  103.4 0.9 copy-done.4
  104.4 82.0 %scatter_sums.1 = (bf16[8,128,256]{2,1,0:T(8,128)(2,1)S(1)}, f32[256,256]{1,0:T(8,128)S(1)}) custom-call(bf16[4,2,8,128,256]{4,3,2,1,0:T(8,128)(2,1)} %bitcast.13, bf16[3,8,128,256]{3,2,1,0:T(8,128)(2,1)S(1)} %copy-done.2, s32[8,8,128]{2,1,0:T(8,128)S(1)} %get-tuple-element.29.tab, f32[256,256]{1,0:T(8,128)S(1)} %copy-done.4), custom_call_target="tpu_custom_call" | custom-call | tf_op jit(solution)/shard_map/scatter_sums/pallas_call | solution.py:524
  186.3 0.8 copy.19
  187.1 0.7 copy.20
Async XLA Ops:
  4.5 1.0 copy-start.3
  5.5 0.7 copy-start.5
  80.9 1.9 %copy-start = (bf16[64,128,256]{2,1,0:T(8,128)(2,1)}, bf16[64,128,256]{2,1,0:T(8,128)(2,1)S(1)}, u32[]{:S(2)}) copy-start(bf16[64,128,256]{2,1,0:T(8,128)(2,1)S(1)} %get-tuple-element.24.pool) | copy-start | bytes 12582916
  82.9 1.2 copy-start.1
  102.0 1.4 copy-start.2
  103.4 0.9 copy-start.4

commit v2 on v0

v2 whole, which is shorter than its diff:
```python
import math

import jax
import jax.numpy as jnp
from jax import lax
from jax.experimental import pallas as pl
from jax.experimental.pallas import tpu as pltpu
from jax.sharding import PartitionSpec as P

MESH = pl.DeviceIdType.MESH
BF = jnp.bfloat16
F32 = jnp.float32
I32 = jnp.int32
NX, NY, NZ = 4, 2, 8
RB, BLK, F = 8, 128, 256
HW = F // 2
N_DOM = 4
KIN, KX = 32, 16
NCROSS = (N_DOM - 1) * KX
W_SCALE = 1.0 / math.sqrt(RB * BLK * NX * NY * NZ * N_DOM)
STRIP = 32
RELS = (0, -1, 1, -2, 2, -3, 3, 4)
SLOT = {rel: i for i, rel in enumerate(RELS)}
SEND, IROW, ISRC, ICOUNT, CROW, CCOL = 0, 1, 2, 3, 8, 11
POS_A, POS_B, POS_C, POS_D, N_POS = 0, 48, 80, 112, 160
KEY_A, KEY_B, KEY_C, KEY_D = 0, 32, 64, 160


def dev_of(x, yh, z):
    return x * 16 + yh * 8 + z


def remote(src, dst, send_sem, recv_sem, dom, dev):
    return pltpu.make_async_remote_copy(
        src_ref=src, dst_ref=dst, send_sem=send_sem, recv_sem=recv_sem,
        device_id=(dom, dev), device_id_type=MESH)


def order_tiles(ints, key_rows, found):
    count = ints[ICOUNT, 0]
    lane = lax.broadcasted_iota(I32, (8, 256), 1)
    keys_lane = jnp.full((8, 256), 9999, I32)

    def put(e, key, keys_lane):
        key_rows[pl.ds(e, 1), :] = jnp.full((1, 256), key, I32)
        return jnp.where(lane == e, key, keys_lane)

    def cross(e, keys_lane):
        o = e // KX
        keys_lane = put(POS_A + e, KEY_A + o * RB + ints[CROW + e // KX, e % KX], keys_lane)
        return put(POS_D + e, KEY_D + o * RB + ints[CCOL + e // KX, e % KX], keys_lane)

    def intra(k, keys_lane):
        keys_lane = put(POS_B + k, KEY_B + jnp.where(k < count, ints[IROW, k], RB), keys_lane)
        return put(POS_C + k, KEY_C + jnp.where(k < count, ints[ISRC, k], NX * NY * NZ), keys_lane)

    keys_lane = lax.fori_loop(0, NCROSS, cross, keys_lane)
    keys_lane = lax.fori_loop(0, KIN, intra, keys_lane)

    def step(t, sums):
        tile, le, eq, skey = sums
        base = pl.multiple_of(t * 8, 8)
        rows = key_rows[pl.ds(base, 8), :]
        sub = base + lax.broadcasted_iota(I32, (8, 256), 0)
        ahead = (keys_lane < rows) | ((keys_lane == rows) & (lane < sub))
        place = jnp.sum(jnp.where(ahead, 1, 0), axis=1, keepdims=True)
        here = place == lane
        tile = tile + jnp.where(here, sub, 0)
        skey = skey + jnp.where(here, rows, 0)
        le = le + jnp.where(rows <= lane, 1, 0)
        eq = eq + jnp.where(rows == lane, 1, 0)
        return tile, le, eq, skey

    zero = jnp.zeros((8, 256), I32)
    tile, le, eq, skey = lax.fori_loop(0, N_POS // 8, step, (zero, zero, zero, zero))
    for r, value in enumerate((tile, le, eq, skey)):
        found[r] = jnp.broadcast_to(jnp.sum(value, axis=0, keepdims=True), (8, 256))


def kernel(ints, ints_vm, feat_hbm, ivals_hbm, cvals_hbm, w, cot_hbm,
           act_hbm, out, wg,
           *scr):
    it = iter(scr)
    feat = next(it)
    own = (next(it), next(it))
    bufs = {0: own}
    for rel in RELS[1:]:
        bufs[rel] = (next(it), next(it))
    (stage, relay, pool, rem_sib, rem_far, rem_sf, ivals, cvals, cot, act, agg, grad, back,
     runs_a, runs_b, key_rows, found, found_sm, tab_vm, tab_sm,
     xbuf, ybuf, part, rin, lin, csums, near, pair, far_in, far_got, wpart, wquarter, wplane, wline,
     loc, meta_s, meta_r, zs, zr, xs, xr, ys, yr, ls, ds, dr,
     bxs, bxr, bls, bys, byr, rs, rr, lts, ltr, bds, bdr, ws, wr) = it
    dom = lax.axis_index("dom")
    dev = lax.axis_index("dev")
    x, yh, z = dev // 16, (dev // 8) % 2, dev % 8
    yo = 1 - yh
    here = x * NY + yh

    def zdev(rel):
        return dev_of(x, yh, (z + rel + NZ) % NZ)

    def xdev(dx):
        return dev_of((x + dx) % NX, yh, z)

    plane = [(dx, dy) for dy in (0, 1) for dx in range(NX) if dx or dy]

    def pdev(dx, dy):
        return dev_of((x + dx) % NX, (yh + dy) % NY, z)

    ydev = dev_of(x, yo, z)
    sib = dom + 1 - 2 * (dom % 2)
    far = (dom + 2) % N_DOM
    sf = (sib + 2) % N_DOM
    doms = (sib, far, sf)

    def o_of(other):
        return (dom - other - 1 + 2 * N_DOM) % N_DOM

    loads = []

    def load(src, dst):
        copy = pltpu.make_async_copy(src, dst, loc.at[len(loads)])
        copy.start()
        loads.append(copy)
        return copy

    to_half = [load(feat_hbm.at[:, :, pl.ds(h * HW, HW)], own[h]) for h in (0, 1)]
    to_feat = load(feat_hbm, feat)
    to_cvals = load(cvals_hbm, cvals)
    to_ivals = load(ivals_hbm, ivals)
    to_cot = load(cot_hbm, cot)

    peers = ([(dom, zdev(rel)) for rel in RELS[1:]] + [(dom, pdev(dx, dy)) for dx, dy in plane]
             + [(d, dev) for d in doms])
    barrier = pltpu.get_barrier_semaphore()
    for d, e in peers:
        pl.semaphore_signal(barrier, inc=1, device_id=(d, e), device_id_type=MESH)
    to_half[0].wait()
    to_half[1].wait()
    pl.semaphore_wait(barrier, len(peers))

    live = []

    def go(copy):
        copy.start()
        live.append(copy)

    def zcopy(src_rel, dst_rel, h):
        s = SLOT[dst_rel] * 2 + h
        to = 1 if dst_rel < 0 or (dst_rel == 4 and h == 0) else -1
        return remote(bufs[src_rel][h], bufs[dst_rel][h], zs.at[s], zr.at[s], dom, zdev(to))

    def zarrived(rel, h):
        zcopy(0, rel, h).wait_recv()

    def meta(rel):
        i = SLOT[-rel] if rel != 4 else SLOT[4]
        return remote(ints_vm.at[pl.ds(0, 8)], tab_vm.at[i], meta_s.at[i], meta_r.at[i], dom, zdev(rel))

    def dcopy(n):
        if n == 0:
            return remote(feat, rem_sib, ds.at[0], dr.at[0], sib, dev)
        if n == 1:
            return remote(feat, rem_far, ds.at[1], dr.at[1], far, dev)
        return remote(rem_far, rem_sf, ds.at[2], dr.at[2], sib, dev)

    def ycopy(rel, h):
        i = SLOT[rel]
        return remote(stage.at[i, h, 0], relay.at[i, h], ys.at[i, h], yr.at[i, h], dom, ydev)

    def serve(rel, h):
        i = SLOT[rel]
        buf = bufs[rel][h]
        zsrc = (z + rel + NZ) % NZ
        for g, y in ((0, yo), (1, yh)):
            for xx in range(NX):
                where = dev_of(xx, y, z)
                pick = ints[SEND, where] if rel == 0 else tab_sm[i, SEND, where]
                stage[i, h, g, xx] = buf[pick]
            if g == 0:
                go(ycopy(rel, h))
        for dx in (1, 2, 3):
            go(remote(stage.at[i, h, 1, (x + dx) % NX], pool.at[h, x, yh, zsrc],
                      xs.at[i, h, 0, dx], xr.at[i, h, 0, dx], dom, xdev(dx)))
        go(pltpu.make_async_copy(stage.at[i, h, 1, x], pool.at[h, x, yh, zsrc], ls.at[i, h, 0]))

    def pass_on(rel, h):
        i = SLOT[rel]
        zsrc = (z + rel + NZ) % NZ
        ycopy(rel, h).wait_recv()
        for dx in (1, 2, 3):
            go(remote(relay.at[i, h, (x + dx) % NX], pool.at[h, x, yo, zsrc],
                      xs.at[i, h, 1, dx], xr.at[i, h, 1, dx], dom, xdev(dx)))
        go(pltpu.make_async_copy(relay.at[i, h, x], pool.at[h, x, yo, zsrc], ls.at[i, h, 1]))

    for h in (0, 1):
        go(zcopy(0, -1, h))
        go(zcopy(0, 1, 1 - h))
    serve(0, 0)
    serve(0, 1)
    for rel in RELS[1:]:
        go(meta(rel))
    to_feat.wait()
    go(dcopy(0))
    go(dcopy(1))

    order_tiles(ints, key_rows, found)
    to_found = load(found, found_sm)
    runs_a[0] = jnp.zeros((BLK, F), F32)
    runs_b[0] = jnp.zeros((BLK, F), F32)

    for rel in RELS[1:]:
        meta(rel).wait_recv()
    tab_vm[0] = ints_vm[:8]
    to_tab = load(tab_vm, tab_sm)
    to_found.wait()
    to_tab.wait()

    def tile_at(i):
        return found_sm[0, 0, i]

    def joined(i, before, product):
        same = (i > 0) & (found_sm[3, 0, i] == found_sm[3, 0, jnp.maximum(i - 1, 0)])
        return product + jnp.where(same, before, 0.0)

    def cross_forward(rem, o, half):
        def step(u4, carry):
            for u in range(4):
                i = o * KX + half * (KX // 2) + u4 * 4 + u
                e = tile_at(POS_A + i)
                product = jnp.dot(cvals[e], rem[ints[CCOL + e // KX, e % KX]], preferred_element_type=F32)
                runs_a[i + 1] = joined(POS_A + i, runs_a[i], product)
            return carry
        lax.fori_loop(0, KX // 8, step, 0)

    to_cvals.wait()
    items = [(s * j, h if s < 0 else 1 - h) for j in (1, 2, 3) for h in (0, 1) for s in (-1, 1)]
    items = [(0, 0), (0, 1)] + items + [(4, 0), (4, 1)]
    LAG = 3
    for n in range(2, len(items) + LAG):
        if n < len(items):
            rel, h = items[n]
            zarrived(rel, h)
            if rel != 4:
                nxt = rel - 1 if rel < 0 else rel + 1
                if nxt == -4 and h == 0:
                    go(zcopy(rel, 4, 0))
                elif nxt == 4 and h == 1:
                    go(zcopy(rel, 4, 1))
                elif abs(nxt) < 4:
                    go(zcopy(rel, nxt, h))
            serve(rel, h)
        if n - LAG >= 0:
            pass_on(*items[n - LAG])
        if n == 4:
            dcopy(0).wait_recv()
        if n == 6:
            dcopy(1).wait_recv()
            go(dcopy(2))
        if n == 9:
            dcopy(2).wait_recv()
        if n in (4, 5):
            cross_forward(rem_sib, o_of(sib), n - 4)
        if n in (7, 8):
            cross_forward(rem_far, o_of(far), n - 7)
        if n in (10, 11):
            cross_forward(rem_sf, o_of(sf), n - 10)

    for rel, h in items:
        i = SLOT[rel]
        for g in (0, 1):
            for dx in (1, 2, 3):
                remote(relay.at[0, 0, 0], pool.at[0, 0, 0, 0], xs.at[i, h, g, dx], xr.at[i, h, g, dx],
                       dom, xdev(dx)).wait_recv()
    for copy in live:
        if copy.is_remote:
            copy.wait_send()
        else:
            copy.wait()
    live.clear()
    to_ivals.wait()
    to_cot.wait()

    def intra_forward(u4, carry):
        for u in range(4):
            i = u4 * 4 + u
            k = tile_at(POS_B + i) - POS_B
            src = ints[ISRC, k]
            sx, sy, sz = src // 16, (src // 8) % 2, src % 8
            picked = jnp.concatenate([pool[0, sx, sy, sz], pool[1, sx, sy, sz]], axis=1)
            product = jnp.dot(ivals[k], picked, preferred_element_type=F32)
            runs_b[i + 1] = joined(POS_B + i, runs_b[i], product)
        return carry
    lax.fori_loop(0, KIN // 4, intra_forward, 0)

    def run_of(runs, key, first):
        last = jnp.maximum(found_sm[1, 0, key] - first, 0)
        return jnp.where(found_sm[2, 0, key] > 0, runs[last], 0.0)

    def dense(r, carry):
        total = run_of(runs_b, KEY_B + r, POS_B)
        for o in range(N_DOM - 1):
            total = total + run_of(runs_a, KEY_A + o * RB + r, POS_A)
        agg_r = total.astype(BF)
        agg[r] = agg_r
        pre = jnp.dot(agg_r, w[...], preferred_element_type=F32)
        sig = jax.nn.sigmoid(pre)
        act[r] = (pre * sig).astype(BF)
        grad_r = (cot[r].astype(F32) * sig * (1.0 + pre * (1.0 - sig))).astype(BF)
        grad[r] = grad_r
        back[r] = lax.dot_general(
            grad_r, w[...], (((1,), (1,)), ((), ())), preferred_element_type=F32).astype(BF)
        return carry
    lax.fori_loop(0, RB, dense, 0)

    turned = (((0,), (0,)), ((), ()))

    def intra_back(u4, carry):
        for u in range(4):
            i = u4 * 4 + u
            k = tile_at(POS_C + i) - POS_C
            product = lax.dot_general(ivals[k], back[ints[IROW, k]], turned, preferred_element_type=F32)
            runs_b[i + 1] = joined(POS_C + i, runs_b[i], product)
        return carry
    lax.fori_loop(0, KIN // 4, intra_back, 0)

    def fill(rel):
        zdst = (z + rel + NZ) % NZ

        def one(c, carry):
            total = run_of(runs_b, KEY_C + (c // NY) * 16 + (c % NY) * 8 + zdst, POS_C).astype(BF)
            pool[0, c // NY, c % NY, zdst] = total[:, :HW]
            pool[1, c // NY, c % NY, zdst] = total[:, HW:]
            return carry
        lax.fori_loop(0, NX * NY, one, 0)

    def bxcopy(rel, h, dx):
        i = SLOT[rel]
        zdst = (z + rel + NZ) % NZ
        return remote(pool.at[h, (x + dx) % NX, :, zdst], xbuf.at[i, h, dx], bxs.at[i, h, dx],
                      bxr.at[i, h, dx], dom, xdev(dx))

    def bown(rel, h):
        i = SLOT[rel]
        zdst = (z + rel + NZ) % NZ
        return pltpu.make_async_copy(pool.at[h, x, :, zdst], xbuf.at[i, h, 0], bls.at[i, h])

    def xsend(rel, h):
        for dx in (1, 2, 3):
            go(bxcopy(rel, h, dx))
        bown(rel, h).start()

    def bycopy(rel, h):
        i = SLOT[rel]
        return remote(xbuf.at[i, h, :, yo], ybuf.at[i, h], bys.at[i, h], byr.at[i, h], dom, ydev)

    def ysend(rel, h):
        for dx in (1, 2, 3):
            bxcopy(rel, h, dx).wait_recv()
        bown(rel, h).wait()
        go(bycopy(rel, h))

    def rcopy(src_rel, j, h):
        return remote(part.at[SLOT[src_rel], h], rin.at[j, h], rs.at[j, h], rr.at[j, h], dom, zdev(1))

    def lcopy(src_rel, j, h):
        return remote(part.at[SLOT[src_rel], h], lin.at[j, h], lts.at[j, h], ltr.at[j, h], dom, zdev(-1))

    def combine(rel, h, extra, store):
        i = SLOT[rel]
        bycopy(rel, h).wait_recv()
        picks = []
        for g, y in ((0, yh), (1, yo)):
            for dx in range(NX):
                d = dev_of((x - dx + NX) % NX, y, z)
                pick = tab_sm[i, SEND, d]
                picks.append((g, dx, [jnp.where(pick == b, 1.0, 0.0).astype(F32) for b in range(RB)]))

        def strip(s, carry):
            rows = pl.ds(pl.multiple_of(s * STRIP, STRIP), STRIP)
            totals = [None] * RB
            for g, dx, on in picks:
                got = (xbuf[i, h, dx, yh, rows] if g == 0 else ybuf[i, h, dx, rows]).astype(F32)
                for b in range(RB):
                    term = got * on[b]
                    totals[b] = term if totals[b] is None else totals[b] + term
            for b in range(RB):
                total = totals[b]
                for ref in extra:
                    total = total + ref[b, rows].astype(F32)
                store(b, rows, total.astype(BF))
            return carry
        lax.fori_loop(0, BLK // STRIP, strip, 0)

    def into_part(rel, h):
        def store(b, rows, value):
            part[SLOT[rel], h, b, rows] = value
        return store

    def cross_back(other):
        o = o_of(other)

        def step(u4, carry):
            for u in range(4):
                i = o * KX + u4 * 4 + u
                e = tile_at(POS_D + i) - POS_D
                product = lax.dot_general(cvals[e], back[ints[CROW + e // KX, e % KX]], turned, preferred_element_type=F32)
                runs_a[i + 1] = joined(POS_D + i, runs_a[i], product)
            return carry
        lax.fori_loop(0, KX // 4, step, 0)

        def one(b, carry):
            csums[o, b] = run_of(runs_a, KEY_D + o * RB + b, POS_D).astype(BF)
            return carry
        lax.fori_loop(0, RB, one, 0)

    wrows = F // N_DOM
    first = dom * wrows + here * 8

    def w_dom(n):
        return remote(wpart.at[pl.ds(doms[n] * wrows, wrows)], wquarter.at[n], ws.at[n], wr.at[n], doms[n], dev)

    def w_plane(n):
        dx, dy = plane[n]
        there = ((x + dx) % NX) * NY + (yh + dy) % NY
        return remote(wquarter.at[3, pl.ds(there * 8, 8)], wplane.at[n], ws.at[3 + n], wr.at[3 + n],
                      dom, pdev(dx, dy))

    def w_line(n):
        return remote(wplane.at[7], wline.at[z], ws.at[10 + n], wr.at[10 + n], dom, zdev(RELS[1 + n]))

    def w_plane_back(n):
        dx, dy = plane[n]
        rows = pl.ds(first, 8)
        return remote(wg.at[rows], wg.at[rows], ws.at[17 + n], wr.at[17 + n], dom, pdev(dx, dy))

    def w_dom_back(n):
        rows = pl.ds(dom * wrows, wrows)
        return remote(wg.at[rows], wg.at[rows], ws.at[24 + n], wr.at[24 + n], doms[n], dev)

    def w_step(step):
        if step == 0:
            wpart[...] = jnp.zeros_like(wpart)

            def add(r, carry):
                wpart[...] += lax.dot_general(agg[r], grad[r], turned, preferred_element_type=F32)
                return carry
            lax.fori_loop(0, RB, add, 0)
            for n in range(3):
                go(w_dom(n))
        if step == 1:
            for n in range(3):
                w_dom(n).wait_recv()
            wquarter[3] = (wpart[pl.ds(dom * wrows, wrows)] + wquarter[0]) + (wquarter[1] + wquarter[2])
            for n in range(7):
                go(w_plane(n))
        if step == 2:
            for n in range(7):
                w_plane(n).wait_recv()
            total = wquarter[3, pl.ds(here * 8, 8)]
            for n in range(7):
                total = total + wplane[n]
            wplane[7] = total
            wline[z] = total
            for n in range(7):
                go(w_line(n))
        if step == 3:
            for n in range(7):
                w_line(n).wait_recv()
            total = wline[0]
            for n in range(1, NZ):
                total = total + wline[n]
            wg[pl.ds(first, 8)] = total * W_SCALE
            for n in range(7):
                go(w_plane_back(n))
        if step == 4:
            for n in range(7):
                w_plane_back(n).wait_recv()
            for n in range(3):
                go(w_dom_back(n))
        if step == 5:
            for n in range(3):
                w_dom_back(n).wait_recv()

    def bd(n):
        if n == 0:
            return remote(csums.at[o_of(sf)], pair, bds.at[0], bdr.at[0], sib, dev)
        if n == 1:
            return remote(csums.at[o_of(sib)], near, bds.at[1], bdr.at[1], sib, dev)
        return remote(far_in, far_got, bds.at[2], bdr.at[2], far, dev)

    turns = [(4, 0), (4, 1)] + [(s * j, h if s > 0 else 1 - h)
                                for j in (3, 2, 1) for h in (0, 1) for s in (1, -1)] + [(0, 0), (0, 1)]
    n_turns = len(turns)
    filled = set()

    def xgo(n):
        if n >= n_turns:
            return
        rel, h = turns[n]
        if rel not in filled:
            filled.add(rel)
            fill(rel)
        xsend(rel, h)

    def finish(n):
        rel, h = turns[n]
        if rel == 4:
            combine(4, h, [], into_part(4, h))
            go(rcopy(4, 3, 0) if h == 0 else lcopy(4, 3, 1))
        elif rel > 0:
            extra = []
            if rel < 3 or h == 0:
                rcopy(4, rel, h).wait_recv()
                extra = [rin.at[rel, h]]
            combine(rel, h, extra, into_part(rel, h))
            go(rcopy(rel, rel - 1, h))
        elif rel < 0:
            extra = []
            if rel > -3 or h == 1:
                lcopy(4, -rel, h).wait_recv()
                extra = [lin.at[-rel, h]]
            combine(rel, h, extra, into_part(rel, h))
            go(lcopy(rel, -rel - 1, h))
        else:
            rcopy(4, 0, h).wait_recv()
            lcopy(4, 0, h).wait_recv()
            cols = pl.ds(h * HW, HW)

            def store(b, rows, value):
                out[b, rows, cols] = value
            combine(0, h, [rin.at[0, h], lin.at[0, h], near.at[:, :, cols], far_got.at[:, :, cols]], store)

    XAHEAD, YAHEAD = 6, 3
    for n in range(XAHEAD):
        xgo(n)
    to_act = load(act, act_hbm)
    w_step(0)
    ysend(*turns[0])
    cross_back(sf)
    go(bd(0))
    ysend(*turns[1])
    cross_back(far)
    for n in range(2, YAHEAD):
        ysend(*turns[n])
    bd(0).wait_recv()

    def add_pair(b, carry):
        far_in[b] = (pair[b].astype(F32) + csums[o_of(far), b].astype(F32)).astype(BF)
        return carry
    lax.fori_loop(0, RB, add_pair, 0)
    go(bd(2))
    for n in range(n_turns):
        xgo(n + XAHEAD)
        if n + YAHEAD < n_turns:
            ysend(*turns[n + YAHEAD])
        if n == n_turns - 2:
            bd(1).wait_recv()
            bd(2).wait_recv()
        finish(n)
        if n == 1:
            cross_back(sib)
            go(bd(1))
        if n in (3, 5, 7, 9):
            w_step((n - 1) // 2)
    w_step(5)
    for copy in live:
        copy.wait_send()
    to_act.wait()


def run(ints, features, intra_vals, cross_vals, weight, cotangent):
    vm = pl.BlockSpec(memory_space=pltpu.VMEM)
    sm = pl.BlockSpec(memory_space=pltpu.SMEM)
    hbm = pl.BlockSpec(memory_space=pl.ANY)
    dma = pltpu.SemaphoreType.DMA
    block = (RB, BLK, F)
    half = (RB, BLK, HW)
    V = pltpu.VMEM
    return pl.pallas_call(
        kernel,
        out_shape=(
            jax.ShapeDtypeStruct(block, BF),
            jax.ShapeDtypeStruct(block, BF),
            jax.ShapeDtypeStruct((F, F), F32),
        ),
        in_specs=[sm, vm, hbm, hbm, hbm, vm, hbm],
        out_specs=(hbm, vm, vm),
        scratch_shapes=[V(block, BF)] + [V(half, BF)] * 16 + [
            V((NZ, 2, NY, NX, BLK, HW), BF),
            V((NZ, 2, NX, BLK, HW), BF),
            V((2, NX, NY, NZ, BLK, HW), BF),
            V(block, BF), V(block, BF), V(block, BF),
            V((KIN, BLK, BLK), BF), V((NCROSS, BLK, BLK), BF),
            V(block, BF), V(block, BF), V(block, BF), V(block, BF), V(block, BF),
            V((NCROSS + 1, BLK, F), F32), V((KIN + 1, BLK, F), F32),
            V((N_POS, 256), I32), V((4, 8, 256), I32), pltpu.SMEM((4, 8, 256), I32),
            V((NZ, 8, 128), I32), pltpu.SMEM((NZ, 8, 128), I32),
            V((NZ, 2, NX, NY, BLK, HW), BF),
            V((NZ, 2, NX, BLK, HW), BF),
            V((NZ, 2) + half, BF),
            V((4, 2) + half, BF), V((4, 2) + half, BF),
            V((N_DOM - 1,) + block, BF),
            V(block, BF), V(block, BF), V(block, BF), V(block, BF),
            V((F, F), F32), V((4, F // N_DOM, F), F32), V((8, 8, F), F32), V((NZ, 8, F), F32),
            dma((9,)), dma((NZ,)), dma((NZ,)),
            dma((2 * NZ,)), dma((2 * NZ,)),
            dma((NZ, 2, 2, 4)), dma((NZ, 2, 2, 4)),
            dma((NZ, 2)), dma((NZ, 2)),
            dma((NZ, 2, 2)),
            dma((3,)), dma((3,)),
            dma((NZ, 2, 4)), dma((NZ, 2, 4)), dma((NZ, 2)),
            dma((NZ, 2)), dma((NZ, 2)),
            dma((4, 2)), dma((4, 2)), dma((4, 2)), dma((4, 2)),
            dma((3,)), dma((3,)),
            dma((27,)), dma((27,)),
        ],
        compiler_params=pltpu.CompilerParams(
            collective_id=0, has_side_effects=True, vmem_limit_bytes=60 << 20),
        name="graph_layer",
    )(ints, ints, features, intra_vals, cross_vals, weight, cotangent)


def deliver_kernel(*refs):
    srcs, dsts, sems = refs[:3], refs[3:6], refs[6]
    copies = [pltpu.make_async_copy(a, b, sems.at[n]) for n, (a, b) in enumerate(zip(srcs, dsts))]
    for copy in copies:
        copy.start()
    for copy in copies:
        copy.wait()


def deliver(*arrays):
    vm = pl.BlockSpec(memory_space=pltpu.VMEM)
    hbm = pl.BlockSpec(memory_space=pl.ANY)
    return pl.pallas_call(
        deliver_kernel,
        out_shape=tuple(jax.ShapeDtypeStruct(a.shape, a.dtype) for a in arrays),
        in_specs=[vm] * 3,
        out_specs=(hbm,) * 3,
        scratch_shapes=[pltpu.SemaphoreType.DMA((3,))],
        name="deliver",
    )(*arrays)


def body(features, weight, cotangent, send_list, intra_rows, intra_src, intra_count, intra_vals,
         cross_rows, cross_cols, cross_vals):
    def placed(row, values):
        flat = values.reshape((-1, values.shape[-1]))
        return jnp.pad(flat, ((row, 16 - row - flat.shape[0]), (0, 128 - flat.shape[1])))

    ints = (placed(SEND, send_list.reshape(1, -1)) + placed(IROW, intra_rows) + placed(ISRC, intra_src)
            + placed(ICOUNT, intra_count) + placed(CROW, cross_rows) + placed(CCOL, cross_cols))
    act, input_grad, weight_grad = run(
        ints, features.reshape(RB, BLK, F), intra_vals[0, 0],
        cross_vals.reshape(NCROSS, BLK, BLK), weight, cotangent.reshape(RB, BLK, F))
    act, input_grad, weight_grad = deliver(act, input_grad, weight_grad)
    return act.reshape(RB * BLK, F), input_grad.reshape(RB * BLK, F), weight_grad


def solution(mesh):
    placed = (
        P(("dom", "dev"), None),
        P(),
        P(("dom", "dev"), None),
        P("dom", "dev", None, None),
        P("dom", "dev", None),
        P("dom", "dev", None),
        P("dom", "dev"),
        P("dom", "dev", None, None, None),
        P("dom", "dev", None, None),
        P("dom", "dev", None, None),
        P("dom", "dev", None, None, None, None),
    )
    return jax.shard_map(
        body,
        mesh=mesh,
        in_specs=placed,
        out_specs=(P(("dom", "dev"), None), P(("dom", "dev"), None), P()),
        check_vma=False,
    )
```

time: 548 us -> 163 us (0.30)
  waiting for transfers between devices: 389 us -> 0 us
  Pallas kernels: 0 us -> 160 us
  other arithmetic: 53.1 us -> 1.3 us
  local copies, waits for them, and re-layouts: 35.9 us -> 0.7 us
  matrix products: 27.9 us -> 0 us
  starting transfers between devices: 25.6 us -> 0 us
  between operations: 15.1 us -> 1.29 us
    psum x1 -> x0, waiting for transfers between devices: 278 us -> none  [body(): weight_sum_all = lax.psum(partial_weight, ('dom', 'dev'))]
    pallas_call x0 -> x2, Pallas kernels: none -> 160 us  [the longest x1 157 us: run(): pl.pallas_call(kernel, out_shape=(jax.ShapeDtypeStruct(block, BF), jax.Sh...]
    ppermute x6 -> x0, waiting for transfers between devices: 63.1 us -> none  [from_behind(): return lax.ppermute(value, axis, pairs)]
    scatter-add x9 -> x0, other arithmetic: 49.7 us -> none  [the longest x3 12.7 us: body(): zero_blocks.at[cross_col[group]].add(cross_out)]
    all_to_all x2 -> x0, waiting for transfers between devices: 48.2 us -> none  [the longest x1 48.2 us: body(): lax.all_to_all(outgoing, 'dev', split_axis=0, concat_axis=0, tiled=True)]
    dot_general x11 -> x0, matrix products: 27.9 us -> none  [the longest x3 8.6 us: body(): jnp.einsum('kab,kbf->kaf', cross_val[cross_group], remote[cross_col[cross...]
    all_to_all x2 -> x0, starting transfers between devices: 20.3 us -> none  [the longest x1 14.1 us: body(): lax.all_to_all(outgoing, 'dev', split_axis=0, concat_axis=0, tiled=True)]
    gather x9 -> x0, local copies, waits for them, and re-layouts: 16.5 us -> none  [the longest x1 4.28 us: body(): slot_pool[tile_source]]
  transfers between devices with their start and end apart: 9 -> 0, of which waited for: 7 -> 0; matrix products, arithmetic and copies ran while one was open for 10% -> 0% of each run, Pallas kernels for 0% -> 0%
where the time goes in v2:
time: 163 us
  Pallas kernels  160 us (98%)
    pallas_call x1, Pallas kernels, run(): pl.pallas_call(kernel, out_shape=(jax.ShapeDtypeStruct(block, BF), jax.Sh...  157 us

profile of v2, /device:TPU:8, one launch (start us, length us, event | category | flops | bytes accessed | tf_op | source)
XLA Modules:
  0.0 163.0 jit_solution(16603851112341757614)
XLA Ops:
  1.3 0.7 copy_bitcast_fusion
  2.0 1.3 pad_add_fusion.ints.ints_vm
  3.3 157.4 %graph_layer.1 = (bf16[8,128,256]{2,1,0:T(8,128)(2,1)}, bf16[8,128,256]{2,1,0:T(8,128)(2,1)}, f32[256,256]{1,0:T(8,128)}) custom-call(s32[16,128]{1,0:T(8,128)} %pad_add_fusion.ints.ints_vm, s32[16,128]{1,0:T(8,128)} %pad_add_fusion.ints.ints_vm, bf16[8,128,256]{2,1,0:T(8,128)(2,1)} %bitcast.15, bf16[32,128,128]{2,1,0:T(8,128)(2,1)} %bitcast.14, ...), custom_call_target="tpu_custom_call" | custom-call | tf_op jit(solution)/shard_map/graph_layer/pallas_call | solution.py:581
  160.6 2.3 %deliver.1 = (bf16[8,128,256]{2,1,0:T(8,128)(2,1)}, bf16[8,128,256]{2,1,0:T(8,128)(2,1)}, f32[256,256]{1,0:T(8,128)}) custom-call(bf16[8,128,256]{2,1,0:T(8,128)(2,1)} %get-tuple-element.9.refs_0_, bf16[8,128,256]{2,1,0:T(8,128)(2,1)} %get-tuple-element.10.refs_1_, f32[256,256]{1,0:T(8,128)} %get-tuple-element.11.refs_2_), custom_call_target="tpu_custom_call" | custom-call | tf_op jit(solution)/shard_map/deliver/pallas_call | solution.py:637

commit v3 on v2

--- a/solution.py
+++ b/solution.py
@@ -86,7 +86,7 @@
     bufs = {0: own}
     for rel in RELS[1:]:
         bufs[rel] = (next(it), next(it))
-    (stage, relay, pool, rem_sib, rem_far, rem_sf, ivals, cvals, cot, act, agg, grad, back,
+    (stage, relay, pool, rem_sib, rem_far0, rem_far1, rem_sf, ivals, cvals, cot, act, agg, grad, back,
      runs_a, runs_b, key_rows, found, found_sm, tab_vm, tab_sm,
      xbuf, ybuf, part, rin, lin, csums, near, pair, far_in, far_got, wpart, wquarter, wplane, wline,
      loc, meta_s, meta_r, zs, zr, xs, xr, ys, yr, ls, ds, dr,
@@ -125,19 +125,18 @@
         loads.append(copy)
         return copy
 
+    peers = ([(dom, zdev(rel)) for rel in RELS[1:]] + [(dom, pdev(dx, dy)) for dx, dy in plane]
+             + [(d, dev) for d in doms] + [(far, ydev)])
+    barrier = pltpu.get_barrier_semaphore()
+    for d, e in peers:
+        pl.semaphore_signal(barrier, inc=1, device_id=(d, e), device_id_type=MESH)
     to_half = [load(feat_hbm.at[:, :, pl.ds(h * HW, HW)], own[h]) for h in (0, 1)]
+    to_half[0].wait()
+    to_half[1].wait()
     to_feat = load(feat_hbm, feat)
     to_cvals = load(cvals_hbm, cvals)
     to_ivals = load(ivals_hbm, ivals)
     to_cot = load(cot_hbm, cot)
-
-    peers = ([(dom, zdev(rel)) for rel in RELS[1:]] + [(dom, pdev(dx, dy)) for dx, dy in plane]
-             + [(d, dev) for d in doms])
-    barrier = pltpu.get_barrier_semaphore()
-    for d, e in peers:
-        pl.semaphore_signal(barrier, inc=1, device_id=(d, e), device_id_type=MESH)
-    to_half[0].wait()
-    to_half[1].wait()
     pl.semaphore_wait(barrier, len(peers))
 
     live = []
@@ -158,12 +157,20 @@
         i = SLOT[-rel] if rel != 4 else SLOT[4]
         return remote(ints_vm.at[pl.ds(0, 8)], tab_vm.at[i], meta_s.at[i], meta_r.at[i], dom, zdev(rel))
 
-    def dcopy(n):
-        if n == 0:
-            return remote(feat, rem_sib, ds.at[0], dr.at[0], sib, dev)
-        if n == 1:
-            return remote(feat, rem_far, ds.at[1], dr.at[1], far, dev)
-        return remote(rem_far, rem_sf, ds.at[2], dr.at[2], sib, dev)
+    rem_far = (rem_far0, rem_far1)
+    halves = [pl.ds(h * HW, HW) for h in (0, 1)]
+
+    def to_sib():
+        return remote(feat, rem_sib, ds.at[0], dr.at[0], sib, dev)
+
+    def to_far(h):
+        return remote(own[h], rem_far[h], ds.at[1 + h], dr.at[1 + h], far, dev)
+
+    def far_to_sib(h):
+        return remote(rem_far[h], rem_sf.at[:, :, halves[h]], ds.at[3 + h], dr.at[3 + h], sib, dev)
+
+    def meta_far():
+        return remote(ints_vm.at[pl.ds(0, 8)], tab_vm.at[NZ], meta_s.at[NZ], meta_r.at[NZ], far, dev)
 
     def ycopy(rel, h):
         i = SLOT[rel]
@@ -194,16 +201,18 @@
                       xs.at[i, h, 1, dx], xr.at[i, h, 1, dx], dom, xdev(dx)))
         go(pltpu.make_async_copy(relay.at[i, h, x], pool.at[h, x, yo, zsrc], ls.at[i, h, 1]))
 
+    for rel in RELS[1:]:
+        go(meta(rel))
+    go(meta_far())
     for h in (0, 1):
         go(zcopy(0, -1, h))
         go(zcopy(0, 1, 1 - h))
     serve(0, 0)
     serve(0, 1)
-    for rel in RELS[1:]:
-        go(meta(rel))
+    go(to_far(0))
+    go(to_far(1))
     to_feat.wait()
-    go(dcopy(0))
-    go(dcopy(1))
+    go(to_sib())
 
     order_tiles(ints, key_rows, found)
     to_found = load(found, found_sm)
@@ -212,6 +221,7 @@
 
     for rel in RELS[1:]:
         meta(rel).wait_recv()
+    meta_far().wait_recv()
     tab_vm[0] = ints_vm[:8]
     to_tab = load(tab_vm, tab_sm)
     to_found.wait()
@@ -224,12 +234,12 @@
         same = (i > 0) & (found_sm[3, 0, i] == found_sm[3, 0, jnp.maximum(i - 1, 0)])
         return product + jnp.where(same, before, 0.0)
 
-    def cross_forward(rem, o, half):
+    def cross_forward(pick, o, half):
         def step(u4, carry):
             for u in range(4):
                 i = o * KX + half * (KX // 2) + u4 * 4 + u
                 e = tile_at(POS_A + i)
-                product = jnp.dot(cvals[e], rem[ints[CCOL + e // KX, e % KX]], preferred_element_type=F32)
+                product = jnp.dot(cvals[e], pick(ints[CCOL + e // KX, e % KX]), preferred_element_type=F32)
                 runs_a[i + 1] = joined(POS_A + i, runs_a[i], product)
             return carry
         lax.fori_loop(0, KX // 8, step, 0)
@@ -253,19 +263,21 @@
             serve(rel, h)
         if n - LAG >= 0:
             pass_on(*items[n - LAG])
+        if n in (3, 5):
+            h = (n - 3) // 2
+            to_far(h).wait_recv()
+            go(far_to_sib(h))
         if n == 4:
-            dcopy(0).wait_recv()
-        if n == 6:
-            dcopy(1).wait_recv()
-            go(dcopy(2))
+            to_sib().wait_recv()
         if n == 9:
-            dcopy(2).wait_recv()
+            far_to_sib(0).wait_recv()
+            far_to_sib(1).wait_recv()
         if n in (4, 5):
-            cross_forward(rem_sib, o_of(sib), n - 4)
+            cross_forward(lambda c: rem_sib[c], o_of(sib), n - 4)
         if n in (7, 8):
-            cross_forward(rem_far, o_of(far), n - 7)
+            cross_forward(lambda c: jnp.concatenate([rem_far0[c], rem_far1[c]], axis=1), o_of(far), n - 7)
         if n in (10, 11):
-            cross_forward(rem_sf, o_of(sf), n - 10)
+            cross_forward(lambda c: rem_sf[c], o_of(sf), n - 10)
 
     for rel, h in items:
         i = SLOT[rel]
@@ -353,7 +365,8 @@
 
     def bycopy(rel, h):
         i = SLOT[rel]
-        return remote(xbuf.at[i, h, :, yo], ybuf.at[i, h], bys.at[i, h], byr.at[i, h], dom, ydev)
+        return remote(xbuf.at[i, h, :, yo], ybuf.at[i, h], bys.at[i, h], byr.at[i, h],
+                      far if rel == 0 else dom, ydev)
 
     def ysend(rel, h):
         for dx in (1, 2, 3):
@@ -367,21 +380,18 @@
     def lcopy(src_rel, j, h):
         return remote(part.at[SLOT[src_rel], h], lin.at[j, h], lts.at[j, h], ltr.at[j, h], dom, zdev(-1))
 
-    def combine(rel, h, extra, store):
-        i = SLOT[rel]
-        bycopy(rel, h).wait_recv()
+    def combine(groups, h, extra, store):
         picks = []
-        for g, y in ((0, yh), (1, yo)):
+        for g, (buf, tab, y) in enumerate(groups):
             for dx in range(NX):
-                d = dev_of((x - dx + NX) % NX, y, z)
-                pick = tab_sm[i, SEND, d]
-                picks.append((g, dx, [jnp.where(pick == b, 1.0, 0.0).astype(F32) for b in range(RB)]))
+                pick = tab_sm[tab, SEND, dev_of((x - dx + NX) % NX, y, z)]
+                picks.append((buf, dx, [jnp.where(pick == b, 1.0, 0.0).astype(F32) for b in range(RB)]))
 
         def strip(s, carry):
             rows = pl.ds(pl.multiple_of(s * STRIP, STRIP), STRIP)
             totals = [None] * RB
-            for g, dx, on in picks:
-                got = (xbuf[i, h, dx, yh, rows] if g == 0 else ybuf[i, h, dx, rows]).astype(F32)
+            for buf, dx, on in picks:
+                got = buf[dx, rows].astype(F32)
                 for b in range(RB):
                     term = got * on[b]
                     totals[b] = term if totals[b] is None else totals[b] + term
@@ -392,6 +402,16 @@
                 store(b, rows, total.astype(BF))
             return carry
         lax.fori_loop(0, BLK // STRIP, strip, 0)
+
+    def own_half(rel, h):
+        return (xbuf.at[SLOT[rel], h, :, yh], SLOT[rel], yh)
+
+    def other_half(rel, h):
+        return (ybuf.at[SLOT[rel], h], SLOT[rel], yo)
+
+    def sum_chunk(rel, h, extra):
+        bycopy(rel, h).wait_recv()
+        combine([own_half(rel, h), other_half(rel, h)], h, extra, into_part(rel, h))
 
     def into_part(rel, h):
         def store(b, rows, value):
@@ -483,45 +503,61 @@
             for n in range(3):
                 w_dom_back(n).wait_recv()
 
-    def bd(n):
+    def bd(n, h=0):
         if n == 0:
             return remote(csums.at[o_of(sf)], pair, bds.at[0], bdr.at[0], sib, dev)
         if n == 1:
             return remote(csums.at[o_of(sib)], near, bds.at[1], bdr.at[1], sib, dev)
-        return remote(far_in, far_got, bds.at[2], bdr.at[2], far, dev)
+        return remote(far_in.at[:, :, halves[h]], far_got.at[:, :, halves[h]], bds.at[2 + h], bdr.at[2 + h],
+                      far, dev)
+
+    def sum_far(h):
+        bycopy(0, h).wait_recv()
+
+        def store(b, rows, value):
+            far_in[b, rows, halves[h]] = value
+        combine([(ybuf.at[0, h], NZ, yo)], h,
+                [pair.at[:, :, halves[h]], csums.at[o_of(far), :, :, halves[h]]], store)
 
     turns = [(4, 0), (4, 1)] + [(s * j, h if s > 0 else 1 - h)
                                 for j in (3, 2, 1) for h in (0, 1) for s in (1, -1)] + [(0, 0), (0, 1)]
     n_turns = len(turns)
+    queue = turns[:6] + [(0, 0), (0, 1)] + turns[6:14]
     filled = set()
-
-    def xgo(n):
-        if n >= n_turns:
-            return
-        rel, h = turns[n]
-        if rel not in filled:
-            filled.add(rel)
-            fill(rel)
-        xsend(rel, h)
+    sent = {"x": 0, "y": 0}
+
+    def xgo(upto):
+        while sent["x"] < min(upto, n_turns):
+            rel, h = queue[sent["x"]]
+            if rel not in filled:
+                filled.add(rel)
+                fill(rel)
+            xsend(rel, h)
+            sent["x"] += 1
+
+    def ygo(upto):
+        while sent["y"] < min(upto, n_turns):
+            ysend(*queue[sent["y"]])
+            sent["y"] += 1
 
     def finish(n):
         rel, h = turns[n]
         if rel == 4:
-            combine(4, h, [], into_part(4, h))
+            sum_chunk(4, h, [])
             go(rcopy(4, 3, 0) if h == 0 else lcopy(4, 3, 1))
         elif rel > 0:
             extra = []
             if rel < 3 or h == 0:
                 rcopy(4, rel, h).wait_recv()
                 extra = [rin.at[rel, h]]
-            combine(rel, h, extra, into_part(rel, h))
+            sum_chunk(rel, h, extra)
             go(rcopy(rel, rel - 1, h))
         elif rel < 0:
             extra = []
             if rel > -3 or h == 1:
                 lcopy(4, -rel, h).wait_recv()
                 extra = [lin.at[-rel, h]]
-            combine(rel, h, extra, into_part(rel, h))
+            sum_chunk(rel, h, extra)
             go(lcopy(rel, -rel - 1, h))
         else:
             rcopy(4, 0, h).wait_recv()
@@ -530,34 +566,32 @@
 
             def store(b, rows, value):
                 out[b, rows, cols] = value
-            combine(0, h, [rin.at[0, h], lin.at[0, h], near.at[:, :, cols], far_got.at[:, :, cols]], store)
-
-    XAHEAD, YAHEAD = 6, 3
-    for n in range(XAHEAD):
-        xgo(n)
+            combine([own_half(0, h)], h, [rin.at[0, h], lin.at[0, h], near.at[:, :, cols], far_got.at[:, :, cols]], store)
+
+    xgo(6)
     to_act = load(act, act_hbm)
     w_step(0)
-    ysend(*turns[0])
+    ygo(1)
     cross_back(sf)
     go(bd(0))
-    ysend(*turns[1])
+    ygo(2)
     cross_back(far)
-    for n in range(2, YAHEAD):
-        ysend(*turns[n])
-    bd(0).wait_recv()
-
-    def add_pair(b, carry):
-        far_in[b] = (pair[b].astype(F32) + csums[o_of(far), b].astype(F32)).astype(BF)
-        return carry
-    lax.fori_loop(0, RB, add_pair, 0)
-    go(bd(2))
+    xgo(8)
+    ygo(3)
     for n in range(n_turns):
-        xgo(n + XAHEAD)
-        if n + YAHEAD < n_turns:
-            ysend(*turns[n + YAHEAD])
+        lead = 4 if n < 3 else 5 if n < 5 else 6
+        xgo(n + lead + 4)
+        ygo(n + lead)
+        if n == 8:
+            bd(0).wait_recv()
+        if n in (8, 9):
+            sum_far(n - 8)
+        if n in (10, 11):
+            go(bd(2, n - 10))
         if n == n_turns - 2:
             bd(1).wait_recv()
-            bd(2).wait_recv()
+        if n >= n_turns - 2:
+            bd(2, n - n_turns + 2).wait_recv()
         finish(n)
         if n == 1:
             cross_back(sib)
@@ -591,12 +625,12 @@
             V((NZ, 2, NY, NX, BLK, HW), BF),
             V((NZ, 2, NX, BLK, HW), BF),
             V((2, NX, NY, NZ, BLK, HW), BF),
-            V(block, BF), V(block, BF), V(block, BF),
+            V(block, BF), V(half, BF), V(half, BF), V(block, BF),
             V((KIN, BLK, BLK), BF), V((NCROSS, BLK, BLK), BF),
             V(block, BF), V(block, BF), V(block, BF), V(block, BF), V(block, BF),
             V((NCROSS + 1, BLK, F), F32), V((KIN + 1, BLK, F), F32),
             V((N_POS, 256), I32), V((4, 8, 256), I32), pltpu.SMEM((4, 8, 256), I32),
-            V((NZ, 8, 128), I32), pltpu.SMEM((NZ, 8, 128), I32),
+            V((NZ + 1, 8, 128), I32), pltpu.SMEM((NZ + 1, 8, 128), I32),
             V((NZ, 2, NX, NY, BLK, HW), BF),
             V((NZ, 2, NX, BLK, HW), BF),
             V((NZ, 2) + half, BF),
@@ -604,16 +638,16 @@
             V((N_DOM - 1,) + block, BF),
             V(block, BF), V(block, BF), V(block, BF), V(block, BF),
             V((F, F), F32), V((4, F // N_DOM, F), F32), V((8, 8, F), F32), V((NZ, 8, F), F32),
-            dma((9,)), dma((NZ,)), dma((NZ,)),
+            dma((9,)), dma((NZ + 1,)), dma((NZ + 1,)),
             dma((2 * NZ,)), dma((2 * NZ,)),
             dma((NZ, 2, 2, 4)), dma((NZ, 2, 2, 4)),
             dma((NZ, 2)), dma((NZ, 2)),
             dma((NZ, 2, 2)),
-            dma((3,)), dma((3,)),
+            dma((5,)), dma((5,)),
             dma((NZ, 2, 4)), dma((NZ, 2, 4)), dma((NZ, 2)),
             dma((NZ, 2)), dma((NZ, 2)),
             dma((4, 2)), dma((4, 2)), dma((4, 2)), dma((4, 2)),
-            dma((3,)), dma((3,)),
+            dma((4,)), dma((4,)),
             dma((27,)), dma((27,)),
         ],
         compiler_params=pltpu.CompilerParams(

time: 163 us -> 160 us (0.982)
  Pallas kernels: 160 us -> 157 us
    pallas_call x1, Pallas kernels: 157 us -> 154 us  [run(): pl.pallas_call(kernel, out_shape=(jax.ShapeDtypeStruct(block, BF), jax.Sh...]
where the time goes in v3:
time: 160 us
  Pallas kernels  157 us (98%)
    pallas_call x1, Pallas kernels, run(): pl.pallas_call(kernel, out_shape=(jax.ShapeDtypeStruct(block, BF), jax.Sh...  154 us

profile of v3, /device:TPU:8, one launch (start us, length us, event | category | flops | bytes accessed | tf_op | source)
XLA Modules:
  0.0 159.8 jit_solution(9177112941989959394)
XLA Ops:
  1.3 0.7 copy_bitcast_fusion
  2.0 1.3 pad_add_fusion.ints.ints_vm
  3.3 154.2 %graph_layer.1 = (bf16[8,128,256]{2,1,0:T(8,128)(2,1)}, bf16[8,128,256]{2,1,0:T(8,128)(2,1)}, f32[256,256]{1,0:T(8,128)}) custom-call(s32[16,128]{1,0:T(8,128)} %pad_add_fusion.ints.ints_vm, s32[16,128]{1,0:T(8,128)} %pad_add_fusion.ints.ints_vm, bf16[8,128,256]{2,1,0:T(8,128)(2,1)} %bitcast.15, bf16[32,128,128]{2,1,0:T(8,128)(2,1)} %bitcast.14, ...), custom_call_target="tpu_custom_call" | custom-call | tf_op jit(solution)/shard_map/graph_layer/pallas_call | solution.py:615
  157.5 2.3 %deliver.1 = (bf16[8,128,256]{2,1,0:T(8,128)(2,1)}, bf16[8,128,256]{2,1,0:T(8,128)(2,1)}, f32[256,256]{1,0:T(8,128)}) custom-call(bf16[8,128,256]{2,1,0:T(8,128)(2,1)} %get-tuple-element.9.refs_0_, bf16[8,128,256]{2,1,0:T(8,128)(2,1)} %get-tuple-element.10.refs_1_, f32[256,256]{1,0:T(8,128)} %get-tuple-element.11.refs_2_), custom_call_target="tpu_custom_call" | custom-call | tf_op jit(solution)/shard_map/deliver/pallas_call | solution.py:671

commit v4 on v3

--- a/solution.py
+++ b/solution.py
@@ -580,7 +580,7 @@
     ygo(3)
     for n in range(n_turns):
         lead = 4 if n < 3 else 5 if n < 5 else 6
-        xgo(n + lead + 4)
+        xgo(n + lead + 3)
         ygo(n + lead)
         if n == 8:
             bd(0).wait_recv()
@@ -596,8 +596,8 @@
         if n == 1:
             cross_back(sib)
             go(bd(1))
-        if n in (3, 5, 7, 9):
-            w_step((n - 1) // 2)
+        if n in (2, 4, 6, 8):
+            w_step(n // 2)
     w_step(5)
     for copy in live:
         copy.wait_send()

time: 160 us -> 159 us (level)
  no operation moved by 1% of the time
where the time goes in v4:
time: 159 us
  Pallas kernels  156 us (98%)
    pallas_call x1, Pallas kernels, run(): pl.pallas_call(kernel, out_shape=(jax.ShapeDtypeStruct(block, BF), jax.Sh...  153 us

profile of v4, /device:TPU:8, one launch (start us, length us, event | category | flops | bytes accessed | tf_op | source)
XLA Modules:
  0.0 158.9 jit_solution(17070569296247386151)
XLA Ops:
  1.3 0.7 copy_bitcast_fusion
  2.0 1.3 pad_add_fusion.ints.ints_vm
  3.3 153.3 %graph_layer.1 = (bf16[8,128,256]{2,1,0:T(8,128)(2,1)}, bf16[8,128,256]{2,1,0:T(8,128)(2,1)}, f32[256,256]{1,0:T(8,128)}) custom-call(s32[16,128]{1,0:T(8,128)} %pad_add_fusion.ints.ints_vm, s32[16,128]{1,0:T(8,128)} %pad_add_fusion.ints.ints_vm, bf16[8,128,256]{2,1,0:T(8,128)(2,1)} %bitcast.15, bf16[32,128,128]{2,1,0:T(8,128)(2,1)} %bitcast.14, ...), custom_call_target="tpu_custom_call" | custom-call | tf_op jit(solution)/shard_map/graph_layer/pallas_call | solution.py:615
  156.6 2.3 %deliver.1 = (bf16[8,128,256]{2,1,0:T(8,128)(2,1)}, bf16[8,128,256]{2,1,0:T(8,128)(2,1)}, f32[256,256]{1,0:T(8,128)}) custom-call(bf16[8,128,256]{2,1,0:T(8,128)(2,1)} %get-tuple-element.9.refs_0_, bf16[8,128,256]{2,1,0:T(8,128)(2,1)} %get-tuple-element.10.refs_1_, f32[256,256]{1,0:T(8,128)} %get-tuple-element.11.refs_2_), custom_call_target="tpu_custom_call" | custom-call | tf_op jit(solution)/shard_map/deliver/pallas_call | solution.py:671
